TPU v7x, 512 devices: a whole 4x8x8 slice. The times are simulated.
512 devices in a mesh: space: 16 (over z_lo, x), wide: 32 (over y, z_hi, core).
Axes of the slice: x: 4, y: 8, z: 8 (z_hi: 2, z_lo: 4; z = z_hi * 4 + z_lo), core: 2. Of those that a mesh axis runs over, the one named last changes fastest.
Arguments:
- latent: bfloat16 [32, 16, 4, 128, 128], P('wide', 'space'), may hold values from -6 to 6
- coords: bfloat16 [32, 16, 4, 2, 128], P('wide', 'space'), may hold values from 0 to 1
- cell_counts: int32 [32, 16, 4], P('wide', 'space'), may hold values from 32 to 128, as said below
- pair_target: int32 [32, 16, 12], P('wide', 'space'), may hold values from 0 to 3, as said below
- pair_source: int32 [32, 16, 12], P('wide', 'space'), may hold values from 0 to 5, as said below
- pair_count: int32 [32, 16], P('wide', 'space'), may hold values from 3 to 12, as said below
- edge_target_w: bfloat16 [128, 128], replicated, may hold values from -0.5 to 0.5
- edge_source_w: bfloat16 [128, 128], replicated, may hold values from -0.5 to 0.5
- edge_offset: float32 [2, 128], replicated, may hold values from -4 to 4
- edge_bias: float32 [128], replicated, may hold values from -4 to 4
- edge_out: bfloat16 [128, 128], replicated, may hold values from -0.0234375 to 0.0234375
- node_in: bfloat16 [256, 128], replicated, may hold values from -0.375 to 0.375
- node_in_bias: float32 [128], replicated, may hold values from -4 to 4
- node_out: bfloat16 [128, 128], replicated, may hold values from -0.5 to 0.5
- node_out_bias: float32 [128], replicated, may hold values from -4 to 4
- norm_gain: float32 [128], replicated, may hold values from 0.25 to 1.75
- cotangent: bfloat16 [32, 16, 4, 128, 128], P('wide', 'space'), may hold values from -6 to 6
Outputs:
- new_latent: bfloat16 [32, 16, 4, 128, 128], P('wide', 'space')
- latent_grad: float32 [32, 16, 4, 128, 128], P('wide', 'space')
- grad_target_w: float32 [128, 128], replicated
- grad_source_w: float32 [128, 128], replicated
- grad_offset: float32 [2, 128], replicated
- grad_bias: float32 [128], replicated
- grad_edge_out: float32 [128, 128], replicated
- grad_node_in: float32 [256, 128], replicated
- grad_in_bias: float32 [128], replicated
- grad_node_out: float32 [128, 128], replicated
- grad_out_bias: float32 [128], replicated
- grad_gain: float32 [128], replicated
Inputs may be any that keep to these rules, and one draw needn't show every extreme that they name: Live particles of a cell are its first cell_counts slots; some cell of the domain is full. The 12 slots of one device name distinct pairs; pair_source - pair_target is 0, 1 or 2, so a source is the target cell, the one before or the one after along the strip. Slots from pair_count on hold valid pairs that are not used. `pair_source`: window index: 0 is the last cell of the previous space index, 1 to 4 the device's own cells, 5 the first cell of the next space index. `pair_count`: each device lists 3, 6 or 12 pairs; some device lists 12.
All inputs are finite; a program needn't handle non-finite values.
Results may differ from a plain program's by a relative error of at most 0.0083.
Values may be sent and summed in bfloat16 or wider, within the bound.
No kernel may reach another device: no remote copies, remote signals or barrier semaphores. Data moves between devices by JAX's collectives and lax.ppermute only.
A program may use at most 64 MiB of HBM per device.

v0:
```python
import math

import jax
import jax.numpy as jnp
from jax import lax
from jax.sharding import PartitionSpec as P


def with_halo(array, sides, width):
    for axis, dim in sides:
        size, length = (lax.axis_size(axis), array.shape[dim])
        up = [(i, (i + 1) % size) for i in range(size - 1)]
        down = [(j, i) for i, j in up]
        last = lax.slice_in_dim(array, length - width, length, axis=dim)
        initial = lax.slice_in_dim(array, 0, width, axis=dim)
        before = lax.ppermute(last, axis, up)
        after = lax.ppermute(initial, axis, down)
        array = jnp.concatenate([before, array, after], axis=dim)
    return array


def from_behind(array, axis, by):
    length = lax.axis_size(axis)
    pairs = [(i, i + by) for i in range(length) if 0 <= i + by < length]
    return lax.ppermute(array, axis, pairs)


def silu_slope(values):
    sigma = jax.nn.sigmoid(values)
    return sigma * (1.0 + values * (1.0 - sigma))


def tile_geometry(own_coords, window_coords, own_live, window_live, target, source):
    target_xy = lax.dynamic_index_in_dim(own_coords, target, 0, False).astype(jnp.float32)
    source_xy = lax.dynamic_index_in_dim(window_coords, source, 0, False).astype(jnp.float32)
    target_live = lax.dynamic_index_in_dim(own_live, target, 0, False).astype(jnp.float32)
    source_live = lax.dynamic_index_in_dim(window_live, source, 0, False).astype(jnp.float32)
    offset_cells = (target - source + 1).astype(jnp.float32)
    delta_x = offset_cells + target_xy[0][:, None] - source_xy[0][None, :]
    delta_y = target_xy[1][:, None] - source_xy[1][None, :]
    falloff = jnp.maximum(1.0 - delta_x * delta_x - delta_y * delta_y, 0.0)
    weight = falloff * falloff * target_live[:, None] * source_live[None, :]
    return (delta_x, delta_y, weight)


def tile_preact(own_proj, window_proj, edge_offset, target, source, delta_x, delta_y):
    target_rows = lax.dynamic_index_in_dim(own_proj, target, 0, False).astype(jnp.float32)
    source_rows = lax.dynamic_index_in_dim(window_proj, source, 0, False).astype(jnp.float32)
    return (
        target_rows[:, None, :]
        + source_rows[None, :, :]
        + delta_x[:, :, None] * edge_offset[0]
        + delta_y[:, :, None] * edge_offset[1]
    )


def edge_forward(
    own_proj,
    window_proj,
    own_coords,
    window_coords,
    own_live,
    window_live,
    targets,
    sources,
    live_pairs,
    slot_stop,
    edge_offset,
):

    def visit(slot_index, running):
        target = targets[slot_index]
        source = sources[slot_index]
        delta_x, delta_y, weight = tile_geometry(
            own_coords, window_coords, own_live, window_live, target, source
        )
        preact = tile_preact(own_proj, window_proj, edge_offset, target, source, delta_x, delta_y)
        active = (slot_index < live_pairs).astype(jnp.float32)
        contrib = jnp.sum(weight[:, :, None] * jax.nn.silu(preact), axis=1) * active
        current = lax.dynamic_index_in_dim(running, target, 0, False)
        return lax.dynamic_update_index_in_dim(running, current + contrib, target, 0)

    return lax.fori_loop(0, slot_stop, visit, jnp.zeros(own_proj.shape, jnp.float32))


def edge_backward(
    own_proj,
    window_proj,
    own_coords,
    window_coords,
    own_live,
    window_live,
    targets,
    sources,
    live_pairs,
    slot_stop,
    edge_offset,
    upstream,
):

    def visit(slot_index, carry):
        grad_own, grad_window, grad_offset = carry
        target = targets[slot_index]
        source = sources[slot_index]
        delta_x, delta_y, weight = tile_geometry(
            own_coords, window_coords, own_live, window_live, target, source
        )
        preact = tile_preact(own_proj, window_proj, edge_offset, target, source, delta_x, delta_y)
        active = (slot_index < live_pairs).astype(jnp.float32)
        upstream_rows = lax.dynamic_index_in_dim(upstream, target, 0, False)
        gated = silu_slope(preact) * weight[:, :, None] * upstream_rows[:, None, :] * active
        own_rows = lax.dynamic_index_in_dim(grad_own, target, 0, False) + jnp.sum(gated, axis=1)
        grad_own = lax.dynamic_update_index_in_dim(grad_own, own_rows, target, 0)
        window_rows = lax.dynamic_index_in_dim(grad_window, source, 0, False) + jnp.sum(
            gated, axis=0
        )
        grad_window = lax.dynamic_update_index_in_dim(grad_window, window_rows, source, 0)
        along = jnp.sum(gated * delta_x[:, :, None], axis=(0, 1))
        across = jnp.sum(gated * delta_y[:, :, None], axis=(0, 1))
        grad_offset = grad_offset + jnp.stack([along, across])
        return (grad_own, grad_window, grad_offset)

    start = (
        jnp.zeros(own_proj.shape, jnp.float32),
        jnp.zeros(window_proj.shape, jnp.float32),
        jnp.zeros(edge_offset.shape, jnp.float32),
    )
    return lax.fori_loop(0, slot_stop, visit, start)


def node_forward(
    flat_rows, aggregate, edge_out, node_in, node_in_bias, node_out, node_out_bias, norm_gain
):
    latent_width = flat_rows.shape[1]
    agg_b = aggregate.astype(jnp.bfloat16)
    message_b = jnp.dot(agg_b, edge_out, preferred_element_type=jnp.float32).astype(jnp.bfloat16)
    hidden_pre = (
        jnp.dot(flat_rows, node_in[:latent_width], preferred_element_type=jnp.float32)
        + jnp.dot(message_b, node_in[latent_width:], preferred_element_type=jnp.float32)
        + node_in_bias
    )
    hidden = jax.nn.silu(hidden_pre)
    hidden_b = hidden.astype(jnp.bfloat16)
    pre_norm = jnp.dot(hidden_b, node_out, preferred_element_type=jnp.float32) + node_out_bias
    row_mean = jnp.mean(pre_norm, axis=-1, keepdims=True)
    centred = pre_norm - row_mean
    row_var = jnp.mean(centred * centred, axis=-1, keepdims=True)
    inverse = lax.rsqrt(row_var + 1e-05)
    normed = centred * inverse
    new_rows = (flat_rows.astype(jnp.float32) + normed * norm_gain).astype(jnp.bfloat16)
    return (new_rows, (agg_b, message_b, hidden_pre, hidden_b, normed, inverse))


def node_backward(flat_rows, cotangent_rows, saved, edge_out, node_in, node_out, norm_gain):
    agg_b, message_b, hidden_pre, hidden_b, normed, inverse = saved
    latent_width = flat_rows.shape[1]
    cotangent_f = cotangent_rows.astype(jnp.float32)
    grad_gain = jnp.sum(cotangent_f * normed, axis=0)
    grad_normed = cotangent_f * norm_gain
    grad_pre = inverse * (
        grad_normed
        - jnp.mean(grad_normed, axis=-1, keepdims=True)
        - normed * jnp.mean(grad_normed * normed, axis=-1, keepdims=True)
    )
    grad_pre_b = grad_pre.astype(jnp.bfloat16)
    grad_out_bias = jnp.sum(grad_pre, axis=0)
    grad_node_out = jnp.dot(hidden_b.T, grad_pre_b, preferred_element_type=jnp.float32)
    grad_hidden = jnp.dot(grad_pre_b, node_out.T, preferred_element_type=jnp.float32) * silu_slope(
        hidden_pre
    )
    grad_hidden_b = grad_hidden.astype(jnp.bfloat16)
    grad_in_bias = jnp.sum(grad_hidden, axis=0)
    grad_node_in = jnp.concatenate(
        [
            jnp.dot(flat_rows.T, grad_hidden_b, preferred_element_type=jnp.float32),
            jnp.dot(message_b.T, grad_hidden_b, preferred_element_type=jnp.float32),
        ],
        axis=0,
    )
    grad_message_b = jnp.dot(
        grad_hidden_b, node_in[latent_width:].T, preferred_element_type=jnp.float32
    ).astype(jnp.bfloat16)
    grad_edge_out = jnp.dot(agg_b.T, grad_message_b, preferred_element_type=jnp.float32)
    grad_aggregate = jnp.dot(grad_message_b, edge_out.T, preferred_element_type=jnp.float32)
    grad_rows = cotangent_f + jnp.dot(
        grad_hidden_b, node_in[:latent_width].T, preferred_element_type=jnp.float32
    )
    return (
        grad_aggregate,
        grad_rows,
        (grad_edge_out, grad_node_in, grad_in_bias, grad_node_out, grad_out_bias, grad_gain),
    )


def on_device(
    latent,
    coords,
    cell_counts,
    pair_target,
    pair_source,
    pair_count,
    edge_target_w,
    edge_source_w,
    edge_offset,
    edge_bias,
    edge_out,
    node_in,
    node_in_bias,
    node_out,
    node_out_bias,
    norm_gain,
    cotangent,
):
    cells, particles, latent_width = latent.shape[2:]
    hidden_width = edge_target_w.shape[1]
    flat_rows = latent.reshape(-1, latent_width)
    own_proj = (
        (jnp.dot(flat_rows, edge_target_w, preferred_element_type=jnp.float32) + edge_bias)
        .astype(jnp.bfloat16)
        .reshape(cells, particles, hidden_width)
    )
    source_proj = (
        jnp.dot(flat_rows, edge_source_w, preferred_element_type=jnp.float32)
        .astype(jnp.bfloat16)
        .reshape(cells, particles, hidden_width)
    )
    live_mask = (
        jnp.arange(particles, dtype=jnp.int32)[None, :] < cell_counts[0, 0][:, None]
    ).astype(jnp.bfloat16)
    own_coords = coords[0, 0]
    end_proj = jnp.concatenate([source_proj[:1], source_proj[-1:]], axis=0)
    end_coords = jnp.concatenate([own_coords[:1], own_coords[-1:]], axis=0)
    end_live = jnp.concatenate([live_mask[:1], live_mask[-1:]], axis=0)
    rim_proj, rim_coords, rim_live = (
        with_halo(end_proj, (("space", 0),), 1),
        with_halo(end_coords, (("space", 0),), 1),
        with_halo(end_live, (("space", 0),), 1),
    )
    window_proj = jnp.concatenate([rim_proj[:1], source_proj, rim_proj[3:]], axis=0)
    window_coords = jnp.concatenate([rim_coords[:1], own_coords, rim_coords[3:]], axis=0)
    window_live = jnp.concatenate([rim_live[:1], live_mask, rim_live[3:]], axis=0)
    targets = pair_target[0, 0]
    sources = pair_source[0, 0]
    live_pairs = pair_count[0, 0]
    aggregate = edge_forward(
        own_proj,
        window_proj,
        own_coords,
        window_coords,
        live_mask,
        window_live,
        targets,
        sources,
        live_pairs,
        targets.shape[0],
        edge_offset,
    )
    new_rows, saved = node_forward(
        flat_rows,
        aggregate.reshape(-1, hidden_width),
        edge_out,
        node_in,
        node_in_bias,
        node_out,
        node_out_bias,
        norm_gain,
    )
    grad_aggregate, grad_rows, node_grads = node_backward(
        flat_rows,
        cotangent.reshape(-1, latent_width),
        saved,
        edge_out,
        node_in,
        node_out,
        norm_gain,
    )
    grad_edge_out, grad_node_in, grad_in_bias, grad_node_out, grad_out_bias, grad_gain = node_grads
    upstream = grad_aggregate.reshape(cells, particles, hidden_width)
    grad_target, grad_window, grad_offset = edge_backward(
        own_proj,
        window_proj,
        own_coords,
        window_coords,
        live_mask,
        window_live,
        targets,
        sources,
        live_pairs,
        targets.shape[0],
        edge_offset,
        upstream,
    )
    from_next = from_behind(grad_window[0].astype(jnp.bfloat16), "space", -1).astype(jnp.float32)
    from_prev = from_behind(grad_window[cells + 1].astype(jnp.bfloat16), "space", 1).astype(
        jnp.float32
    )
    grad_source = grad_window[1 : cells + 1].at[cells - 1].add(from_next).at[0].add(from_prev)
    target_flat = grad_target.reshape(-1, hidden_width)
    target_b = target_flat.astype(jnp.bfloat16)
    source_b = grad_source.reshape(-1, hidden_width).astype(jnp.bfloat16)
    grad_target_w = jnp.dot(flat_rows.T, target_b, preferred_element_type=jnp.float32)
    grad_source_w = jnp.dot(flat_rows.T, source_b, preferred_element_type=jnp.float32)
    grad_bias = jnp.sum(target_flat, axis=0)
    grad_rows = (
        grad_rows
        + jnp.dot(target_b, edge_target_w.T, preferred_element_type=jnp.float32)
        + jnp.dot(source_b, edge_source_w.T, preferred_element_type=jnp.float32)
    )
    summed = list(
        lax.psum(
            (
                grad_target_w,
                grad_source_w,
                grad_offset,
                grad_bias,
                grad_edge_out,
                grad_node_in,
                grad_in_bias,
                grad_node_out,
                grad_out_bias,
                grad_gain,
            ),
            ("space", "wide"),
        )
    )
    grad_scale = 1.0 / math.sqrt(lax.axis_size("space") * lax.axis_size("wide") * cells * particles)
    scaled = [member * grad_scale for member in summed]
    return (
        new_rows.reshape(latent.shape),
        grad_rows.reshape(latent.shape),
        scaled[0],
        scaled[1],
        scaled[2],
        scaled[3],
        scaled[4],
        scaled[5],
        scaled[6],
        scaled[7],
        scaled[8],
        scaled[9],
    )


def solution(mesh):
    placed = (
        P("wide", "space", None, None, None),
        P("wide", "space", None, None, None),
        P("wide", "space", None),
        P("wide", "space", None),
        P("wide", "space", None),
        P("wide", "space"),
        P(),
        P(),
        P(),
        P(),
        P(),
        P(),
        P(),
        P(),
        P(),
        P(),
        P("wide", "space", None, None, None),
    )
    return jax.shard_map(
        on_device,
        mesh=mesh,
        in_specs=placed,
        out_specs=(
            P("wide", "space", None, None, None),
            P("wide", "space", None, None, None),
            P(),
            P(),
            P(),
            P(),
            P(),
            P(),
            P(),
            P(),
            P(),
            P(),
        ),
        check_vma=False,
    )
```

profile of v0, /device:TPU:1, one launch (start us, length us, event | category | flops | bytes accessed | tf_op | source)
XLA Modules:
  0.0 792.9 jit_solution(4024216699989142781)
XLA Ops:
  8.0 3.9 collective-permute-start
  11.9 1.3 collective-permute-start.1
  14.0 4.0 collective-permute-start.2
  17.9 1.3 collective-permute-start.3
  19.3 1.1 convolution_convert_fusion.2
  20.4 4.0 collective-permute-start.4
  25.0 1.3 collective-permute-start.5
  26.4 3.3 collective-permute-done.5
  29.8 173.8 %while.33 = (s32[]{:T(128)}, f32[4,128,128]{2,1,0:T(8,128)S(1)}, s32[12]{0:T(128)S(1)}, s32[12]{0:T(128)S(1)}, bf16[4,2,128]{2,1,0:T(2,128)(2,1)S(1)}, /*index=5...) while((s32[]{:T(128)}, f32[4,128,128]{2,1,0:T(8,128)S(1)}, ...), condition=%wide.region_2.3_spmd, body=%wide.region_0.2_spmd.sunk | while | flops 23282572 | bytes 998219 | solution.py:83
  37.0 7.2 multiply_reduce_fusion.8
  51.5 7.2 multiply_reduce_fusion.8
  66.0 7.2 multiply_reduce_fusion.8
  80.5 7.2 multiply_reduce_fusion.8
  95.0 7.2 multiply_reduce_fusion.8
  109.5 7.2 multiply_reduce_fusion.8
  124.0 7.2 multiply_reduce_fusion.8
  138.4 7.2 multiply_reduce_fusion.8
  152.9 7.2 multiply_reduce_fusion.8
  167.4 7.2 multiply_reduce_fusion.8
  181.9 7.2 multiply_reduce_fusion.8
  196.4 7.2 multiply_reduce_fusion.8
  206.1 1.0 fusion.31
  207.1 0.9 fusion.22
  208.9 0.9 fusion.37
  210.2 180.3 %while.34 = (s32[]{:T(128)}, f32[4,128,128]{2,1,0:T(8,128)S(1)}, f32[6,128,128]{2,1,0:T(8,128)S(1)}, f32[2,128]{1,0:T(2,128)S(1)}, s32[12]{0:T(128)S(1)}, /*inde...) while((s32[]{:T(128)}, f32[4,128,128]{2,1,0:T(8,128)S(1)}, ...), condition=%wide.region_12.13_spmd.clone, body=%wide.region_7.12_spmd.clone.sunk | while | flops 44238220 | bytes 1461109 | solution.py:128
  217.5 7.6 multiply_reduce_fusion.9
  232.6 7.6 multiply_reduce_fusion.9
  247.6 7.6 multiply_reduce_fusion.9
  262.6 7.6 multiply_reduce_fusion.9
  277.6 7.6 multiply_reduce_fusion.9
  292.6 7.6 multiply_reduce_fusion.9
  307.7 7.6 multiply_reduce_fusion.9
  322.7 7.6 multiply_reduce_fusion.9
  337.7 7.6 multiply_reduce_fusion.9
  352.7 7.6 multiply_reduce_fusion.9
  367.8 7.6 multiply_reduce_fusion.9
  382.8 7.6 multiply_reduce_fusion.9
  390.6 0.9 convolution_bitcast_fusion.2
  391.6 112.0 %all-reduce = (f32[2,128]{1,0:T(2,128)S(1)}, f32[128]{0:T(128)S(1)}, f32[128]{0:T(128)S(1)}, f32[128]{0:T(128)S(1)}, f32[128]{0:T(128)S(1)}) all-reduce(f32[2,128]{1,0:T(2,128)S(1)} %get-tuple-element.484, f32[128]{0:T(128)S(1)} %get-tuple-element.658, ...), channel_id=1, replica_groups=mesh['space'=16,'wide'=32] {'space','wide'}, use_global_device_ids=true, to_apply=%region_15.16 | all-reduce | flops 768 | bytes 6144 | tf_op jit(solution)/shard_map/psum | solution.py:310
  504.2 1.6 collective-permute-start.7
  505.9 1.3 collective-permute-start.6
  508.9 1.6 collective-permute-done.6
  510.6 0.9 convolution_bitcast_fusion.1
  511.5 0.9 convolution_add_fusion
  512.4 269.1 %all-reduce.4.cloned.1.call-done = (f32[128,128]{0,1:T(8,128)}, f32[128,128]{0,1:T(8,128)}, f32[128,128]{0,1:T(8,128)}, f32[256,128]{1,0:T(8,128)}, f32[128,128]{0,1:T(8,128)}) async-done(((f32[128,128]{0,1:T(8,128)}, f32[128,128]{0,1:T(8,128)}, f32[128,128]{0,1:T(8,128)}, f32[256,128]{1,0:T(8,128)}, f32[128,128]{0,1:T(8,128)}), (f32[128,128]{0,1:T(8,128)}, f32[128,128]{0,1:T(8,128)}, f32[128,128]{0,1:T(8,128)}, ...) | async-done | bytes 393232 | tf_op jit(solution)/shard_map/psum | solution.py:310
  781.5 0.9 broadcast_multiply_fusion.3
  782.4 0.7 copy.38
  784.6 0.7 copy.40
  (390 shorter events, 44.3 us)
Async XLA Ops:
  7.2 197.6 %copy-start = (bf16[128,128]{1,0:T(8,128)(2,1)S(1)}, bf16[128,128]{1,0:T(8,128)(2,1)}, u32[]{:S(2)}) copy-start(bf16[128,128]{1,0:T(8,128)(2,1)} %param.38) | copy-start | bytes 98308
  7.2 17.2 %copy-start.1 = (bf16[1,1,4,128,128]{4,3,2,1,0:T(8,128)(2,1)S(1)}, bf16[1,1,4,128,128]{4,3,2,1,0:T(8,128)(2,1)}, u32[]{:S(2)}) copy-start(bf16[1,1,4,128,128]{4,3,2,1,0:T(8,128)(2,1)} %param.25) | copy-start | bytes 393220
  7.2 17.2 %copy-start.3 = (bf16[256,128]{1,0:T(8,128)(2,1)S(1)}, bf16[256,128]{1,0:T(8,128)(2,1)}, u32[]{:S(2)}) copy-start(bf16[256,128]{1,0:T(8,128)(2,1)} %param.36) | copy-start | bytes 196612
  7.2 774.3 %all-reduce.4.cloned.1.call-start = ((), (), s32[]{:S(2)}) async-start(), calls=%async_computation | async-start | bytes 786432 | tf_op jit(solution)/shard_map/psum | solution.py:310
  8.0 18.4 %collective-permute-start = (bf16[1,2,128]{2,1,0:T(2,128)(2,1)S(1)}, bf16[1,2,128]{2,1,0:T(2,128)(2,1)S(1)}, u32[]{:S(2)}, u32[]{:S(2)}) collective-permute-start(bf16[1,2,128]{2,1,0:T(2,128)(2,1)S(1)} %get-tuple-element.664), channel_id=1, source_target_pairs={{0,32},{32,64},{64,96},{96,128},{128,160},{160,192},{192,224},{224... | collective-permute-start | bytes 1544 | tf_op jit(solution)/shard_map/ppermute | solution.py:16
  11.9 14.5 %collective-permute-start.1 = (bf16[1,2,128]{2,1,0:T(2,128)(2,1)S(1)}, bf16[1,2,128]{2,1,0:T(2,128)(2,1)S(1)}, u32[]{:S(2)}, u32[]{:S(2)}) collective-permute-start(bf16[1,2,128]{2,1,0:T(2,128)(2,1)S(1)} %get-tuple-element.665), channel_id=1, source_target_pairs={{32,0},{64,32},{96,64},{128,96},{160,128},{192,160},{224,192},{256... | collective-permute-start | bytes 1544 | tf_op jit(solution)/shard_map/ppermute | solution.py:17
  14.0 11.1 %collective-permute-start.2 = (bf16[1,128]{1,0:T(2,128)(2,1)S(1)}, bf16[1,128]{1,0:T(2,128)(2,1)S(1)}, u32[]{:S(2)}, u32[]{:S(2)}) collective-permute-start(bf16[1,128]{1,0:T(2,128)(2,1)S(1)} %get-tuple-element.666), channel_id=1, source_target_pairs={{0,32},{32,64},{64,96},{96,128},{128,160},{160,192},{192,224},{224... | collective-permute-start | bytes 776 | tf_op jit(solution)/shard_map/ppermute | solution.py:16
  17.9 8.4 %collective-permute-start.3 = (bf16[1,128]{1,0:T(2,128)(2,1)S(1)}, bf16[1,128]{1,0:T(2,128)(2,1)S(1)}, u32[]{:S(2)}, u32[]{:S(2)}) collective-permute-start(bf16[1,128]{1,0:T(2,128)(2,1)S(1)} %get-tuple-element.667), channel_id=1, source_target_pairs={{32,0},{64,32},{96,64},{128,96},{160,128},{192,160},{224,192},{256... | collective-permute-start | bytes 776 | tf_op jit(solution)/shard_map/ppermute | solution.py:17
  19.2 5.4 copy-start.2
  19.2 5.4 copy-start.12
  20.4 4.4 copy-start.6
  20.4 4.4 copy-start.13
  20.4 6.0 copy-start.11
  20.4 6.0 collective-permute-start.4
  25.0 4.8 copy-start.8
  25.0 4.8 copy-start.16
  25.0 4.8 copy-start.17
  25.0 4.7 collective-permute-start.5
  203.6 0.8 copy-start.5
  203.6 0.9 copy-start.14
  204.6 0.7 copy-start.15
  504.2 6.3 collective-permute-start.7
  505.9 4.7 collective-permute-start.6
  510.6 0.9 copy-start.7
  781.5 2.4 copy-start.4
  781.5 3.1 copy-start.9
  781.5 3.1 copy-start.10
Sparse Core Ops, SparseCore 0:
  511.6 269.8 all-reduce.3
where the time goes:
time: 795 us; the launch traced here: 793 us
  waiting for transfers between devices  274 us (34%)
  other arithmetic  190 us (24%)
  loops' own time  142 us (18%)
  blocking collectives  112 us (14%)
  local copies, waits for them, and re-layouts  33.6 us (4%)
  starting transfers between devices  18.7 us (2%)
  between operations  14.6 us (2%)
    psum x1, waiting for transfers between devices, on_device(): lax.psum((grad_target_w, grad_source_w, grad_offset, grad_bias, grad_edge...  269 us
    psum x1, blocking collectives, on_device(): lax.psum((grad_target_w, grad_source_w, grad_offset, grad_bias, grad_edge...  112 us
    reduce_sum x12, other arithmetic, visit(): along = jnp.sum(gated * delta_x[:, :, None], axis=(0, 1))  91.7 us
    reduce_sum x12, other arithmetic, visit(): contrib = jnp.sum(weight[:, :, None] * jax.nn.silu(preact), axis=1) * active  86.4 us
    another operation x1, loops' own time, edge_backward(): return lax.fori_loop(0, slot_stop, visit, start)  71.3 us
    another operation x1, loops' own time, edge_forward(): lax.fori_loop(0, slot_stop, visit, jnp.zeros(own_proj.shape, jnp.float32))  71 us
  transfers between devices with their start and end apart: 9, of which 3 were waited for; matrix products, arithmetic and copies ran while one was open for 1% of the time, Pallas kernels for 0%

commit v1 on v0

v1 whole, which is shorter than its diff:
```python
import functools
import math

import jax
import jax.numpy as jnp
from jax import lax
from jax.experimental import pallas as pl
from jax.experimental.pallas import tpu as pltpu
from jax.sharding import PartitionSpec as P

BF = jnp.bfloat16
F32 = jnp.float32
META = 16
GRAIN = 16
PACK_ROWS = 800


def dot(a, b):
    return jnp.dot(a, b, preferred_element_type=F32)


def dot_t(a, b):
    return lax.dot_general(a, b, (((1,), (1,)), ((), ())), preferred_element_type=F32)


def t_dot(a, b):
    return lax.dot_general(a, b, (((0,), (0,)), ((), ())), preferred_element_type=F32)


def sigmoid(v):
    return 0.5 * (1.0 + jnp.tanh(0.5 * v))


def blocks(count):
    return lax.div(count + (GRAIN - 1), GRAIN)


def column_sum(values):
    return jnp.sum(values, axis=0, keepdims=True)


def step_kernel(
    counts_ref,
    targets_ref,
    sources_ref,
    listed_ref,
    latent_ref,
    meta_ref,
    before_ref,
    after_ref,
    target_w_ref,
    source_w_ref,
    offset_ref,
    bias_ref,
    edge_out_ref,
    node_in_ref,
    node_in_bias_ref,
    node_out_ref,
    node_out_bias_ref,
    gain_ref,
    cotangent_ref,
    new_latent_ref,
    latent_grad_ref,
    rim_grad_ref,
    pack_ref,
    live_ref,
    place_ref,
    x_ref,
    y_ref,
    a_base_ref,
    b_base_ref,
    weight_ref,
    weight_t_ref,
    aggregate_ref,
    slope_ref,
    slope_shift_ref,
    upstream_ref,
    source_grad_ref,
    a_ref,
    a_half_ref,
    b_ref,
    b_half_ref,
    pair_sum_ref,
    shift_ref,
):
    cells, particles, width = latent_ref.shape[2:]
    rows = cells * particles
    offset_x = offset_ref[0:1, :]
    offset_y = offset_ref[1:2, :]

    for cell in range(cells):
        live_ref[cell + 1] = counts_ref[0, 0, cell]
        place_ref[cell + 1] = meta_ref[cell].astype(F32)
    place_ref[0] = before_ref[particles:, :].astype(F32)
    place_ref[cells + 1] = after_ref[particles:, :].astype(F32)
    live_ref[0] = jnp.sum(place_ref[0, 2:3, :]).astype(jnp.int32)
    live_ref[cells + 1] = jnp.sum(place_ref[cells + 1, 2:3, :]).astype(jnp.int32)

    pick = lax.broadcasted_iota(jnp.int32, (META, width), 0)
    pick_x = jnp.where(pick == 0, 1.0, 0.0).astype(BF)
    pick_y = jnp.where(pick == 1, 1.0, 0.0).astype(BF)
    for slot in range(cells + 2):
        if slot == 0:
            rows_in = before_ref[:particles, :]
        elif slot == cells + 1:
            rows_in = after_ref[:particles, :]
        else:
            rows_in = latent_ref[0, 0, slot - 1]
        place = place_ref[slot].astype(BF)
        x = t_dot(place, pick_x)
        y = t_dot(place, pick_y)
        x_ref[slot] = x
        y_ref[slot] = y
        moved = x * offset_x + (y - 0.5) * offset_y
        proj_source = dot(rows_in, source_w_ref[...]).astype(BF).astype(F32)
        b_base_ref[slot] = 0.5 * (proj_source - moved)
        if 0 < slot < cells + 1:
            proj_target = (dot(rows_in, target_w_ref[...]) + bias_ref[...]).astype(BF)
            a_base_ref[slot - 1] = 0.5 * (proj_target.astype(F32) + moved)

    aggregate_ref[...] = jnp.zeros_like(aggregate_ref)
    slope_ref[...] = jnp.zeros_like(slope_ref)
    slope_shift_ref[...] = jnp.zeros_like(slope_shift_ref)
    source_grad_ref[...] = jnp.zeros_like(source_grad_ref)
    shift_ref[...] = jnp.zeros_like(shift_ref)

    row_of = lax.broadcasted_iota(jnp.int32, (GRAIN, width), 0)
    sub = lax.broadcasted_iota(jnp.int32, (particles, particles), 0)
    lane = lax.broadcasted_iota(jnp.int32, (particles, particles), 1)
    listed = listed_ref[0, 0]

    def pair_of(slot):
        target = targets_ref[0, 0, slot]
        source = sources_ref[0, 0, slot]
        off = (target - source + 1).astype(F32)
        alpha = jnp.where(off < -0.5, -1.0, jnp.where(off > 0.5, 0.0, -0.5))
        return target, source, off, alpha, off - alpha

    def set_pair(target, source, alpha, beta):
        a = a_base_ref[target] + (0.5 * alpha) * offset_x
        b = b_base_ref[source] + (0.5 * beta) * offset_x
        a_ref[...] = a
        b_ref[...] = b
        a_half_ref[...] = a.astype(BF)
        b_half_ref[...] = b.astype(BF)

    def over_sizes(count, visit):
        for size in range(2 * GRAIN, particles + 1, GRAIN):
            pl.when(blocks(count) == size // GRAIN)(functools.partial(visit, size))

    def forward_pair(slot, _):
        target, source, off, alpha, beta = pair_of(slot)
        live_target = live_ref[target + 1]
        live_source = live_ref[source]

        @pl.when(live_source > 0)
        def _():
            set_pair(target, source, alpha, beta)
            dx = (off + x_ref[target + 1]) - place_ref[source, 0:1, :]
            dy = y_ref[target + 1] - place_ref[source, 1:2, :]
            near = jnp.maximum(1.0 - dx * dx - dy * dy, 0.0)
            keep = (sub < live_target) & (lane < live_source)
            weight = jnp.where(keep, near * near, 0.0).astype(BF)
            weight_ref[slot] = weight
            dx = (off + place_ref[target + 1, 0:1, :]) - x_ref[source]
            dy = place_ref[target + 1, 1:2, :] - y_ref[source]
            near = jnp.maximum(1.0 - dx * dx - dy * dy, 0.0)
            keep = (lane < live_target) & (sub < live_source)
            weight_t_ref[slot] = jnp.where(keep, near * near, 0.0).astype(BF)
            ones = jnp.ones((particles, width), BF)
            linear = dot(weight, jnp.concatenate([b_half_ref[...], ones], axis=1))
            weight_sum = linear[:, width:]
            aggregate_ref[target] += a_ref[...] * weight_sum + linear[:, :width]
            pair_sum_ref[...] = weight_sum

            def visit(size):
                def block(index, _):
                    first = pl.multiple_of(index * GRAIN, GRAIN)
                    here = pl.ds(first, GRAIN)
                    weights = weight_ref[slot, here, :]
                    b = b_half_ref[0:size, :]
                    total = jnp.zeros((GRAIN, 2 * width), F32)
                    for r in range(GRAIN):
                        a = a_ref[pl.ds(first + r, 1), :].astype(BF)
                        u = jnp.broadcast_to(a, (size, width)) + b
                        t = jnp.tanh(u)
                        bent = u * t
                        steep = t + u * (1.0 - t * t)
                        one = jnp.where(row_of == r, weights, jnp.zeros_like(weights))
                        total = total + dot(
                            one[:, :size], jnp.concatenate([bent, steep], axis=1)
                        )
                    aggregate_ref[target, here, :] += total[:, :width]
                    pair_sum_ref[here, :] += total[:, width:]
                    return 0

                lax.fori_loop(0, blocks(live_target), block, 0)

            over_sizes(live_source, visit)
            slope_ref[target] += pair_sum_ref[...]
            slope_shift_ref[target] += alpha * pair_sum_ref[...]

        return 0

    lax.fori_loop(0, listed, forward_pair, 0)

    latent = latent_ref[0, 0].reshape(rows, width)
    agg_b = aggregate_ref[...].reshape(rows, width).astype(BF)
    message = dot(agg_b, edge_out_ref[...]).astype(BF)
    hidden_pre = (
        dot(latent, node_in_ref[:width, :])
        + dot(message, node_in_ref[width:, :])
        + node_in_bias_ref[...]
    )
    gate = sigmoid(hidden_pre)
    hidden_b = (hidden_pre * gate).astype(BF)
    pre_norm = dot(hidden_b, node_out_ref[...]) + node_out_bias_ref[...]
    centred = pre_norm - jnp.mean(pre_norm, axis=-1, keepdims=True)
    inverse = lax.rsqrt(jnp.mean(centred * centred, axis=-1, keepdims=True) + 1e-05)
    normed = centred * inverse
    gain = gain_ref[...]
    new_rows = (latent.astype(F32) + normed * gain).astype(BF)
    new_latent_ref[0, 0] = new_rows.reshape(cells, particles, width)

    cotangent = cotangent_ref[0, 0].reshape(rows, width).astype(F32)
    gain_sum = column_sum(cotangent * normed)
    scaled = cotangent * gain
    grad_pre = inverse * (
        scaled
        - jnp.mean(scaled, axis=-1, keepdims=True)
        - normed * jnp.mean(scaled * normed, axis=-1, keepdims=True)
    )
    grad_pre_b = grad_pre.astype(BF)
    out_bias_sum = column_sum(grad_pre)
    pack_ref[640:768, :] = t_dot(hidden_b, grad_pre_b).astype(BF)
    grad_hidden = dot_t(grad_pre_b, node_out_ref[...]) * (
        gate * (1.0 + hidden_pre * (1.0 - gate))
    )
    grad_hidden_b = grad_hidden.astype(BF)
    in_bias_sum = column_sum(grad_hidden)
    pack_ref[384:512, :] = t_dot(latent, grad_hidden_b).astype(BF)
    pack_ref[512:640, :] = t_dot(message, grad_hidden_b).astype(BF)
    grad_message = dot_t(grad_hidden_b, node_in_ref[width:, :]).astype(BF)
    pack_ref[256:384, :] = t_dot(agg_b, grad_message).astype(BF)
    upstream = dot_t(grad_message, edge_out_ref[...])
    upstream_ref[...] = upstream.reshape(cells, particles, width)
    grad_rows = cotangent + dot_t(grad_hidden_b, node_in_ref[:width, :])
    latent_grad_ref[0, 0] = grad_rows.reshape(cells, particles, width)

    def backward_pair(slot, _):
        target, source, _, alpha, beta = pair_of(slot)
        live_target = live_ref[target + 1]
        live_source = live_ref[source]

        @pl.when(live_source > 0)
        def _():
            set_pair(target, source, alpha, beta)
            pair_sum_ref[...] = dot(weight_t_ref[slot], upstream_ref[target].astype(BF))

            def visit(size):
                def block(index, _):
                    first = pl.multiple_of(index * GRAIN, GRAIN)
                    here = pl.ds(first, GRAIN)
                    weights = weight_t_ref[slot, here, :][:, :size]
                    a = a_half_ref[0:size, :]
                    up = upstream_ref[target, 0:size, :].astype(BF)

                    def steep(r):
                        b = b_ref[pl.ds(first + r, 1), :].astype(BF)
                        u = jnp.broadcast_to(b, (size, width)) + a
                        t = jnp.tanh(u)
                        return up * (t + u * (1.0 - t * t))

                    total = jnp.zeros((GRAIN, width), F32)
                    for r in range(0, GRAIN, 2):
                        both = dot(weights, jnp.concatenate([steep(r), steep(r + 1)], axis=1))
                        total = jnp.where(row_of == r, both[:, :width], total)
                        total = jnp.where(row_of == r + 1, both[:, width:], total)
                    pair_sum_ref[here, :] += total
                    return 0

                lax.fori_loop(0, blocks(live_source), block, 0)

            over_sizes(live_target, visit)
            grads = 0.5 * pair_sum_ref[...]
            source_grad_ref[source] += grads
            shift_ref[...] += beta * jnp.sum(grads.reshape(particles // 8, 8, width), axis=0)

        return 0

    lax.fori_loop(0, listed, backward_pair, 0)

    upstream = upstream_ref[...].reshape(rows, width)
    target_grad = 0.5 * upstream * slope_ref[...].reshape(rows, width)
    target_b = target_grad.astype(BF)
    source_grad = source_grad_ref[...].reshape(rows + 2 * particles, width)
    source_b = source_grad.astype(BF)
    own_b = source_b[particles : particles + rows]
    rim_grad_ref[0] = source_b[:particles]
    rim_grad_ref[1] = source_b[particles + rows :]
    latent = latent_ref[0, 0].reshape(rows, width)
    pack_ref[0:128, :] = t_dot(latent, target_b).astype(BF)
    pack_ref[128:256, :] = (
        t_dot(latent, own_b)
        + t_dot(before_ref[:particles, :], source_b[:particles])
        + t_dot(after_ref[:particles, :], source_b[particles + rows :])
    ).astype(BF)
    more = dot_t(target_b, target_w_ref[...]) + dot_t(own_b, source_w_ref[...])
    latent_grad_ref[0, 0] += more.reshape(cells, particles, width)
    x_target = x_ref[1 : cells + 1].reshape(rows, width)
    y_target = y_ref[1 : cells + 1].reshape(rows, width)
    x_source = x_ref[...].reshape(rows + 2 * particles, width)
    y_source = y_ref[...].reshape(rows + 2 * particles, width)
    shift = 0.5 * upstream * slope_shift_ref[...].reshape(rows, width)
    along = (
        column_sum(x_target * target_grad + shift)
        - column_sum(x_source * source_grad)
        + column_sum(shift_ref[...])
    )
    across = column_sum((y_target - 0.5) * target_grad) - column_sum((y_source - 0.5) * source_grad)
    small = jnp.concatenate(
        [
            along,
            across,
            column_sum(target_grad),
            in_bias_sum,
            out_bias_sum,
            gain_sum,
            jnp.zeros((2, width), F32),
        ],
        axis=0,
    )
    coarse = small.astype(BF).astype(F32)
    pack_ref[768:784, :] = jnp.concatenate([coarse, small - coarse], axis=0).astype(BF)
    pack_ref[784:800, :] = jnp.zeros((16, width), BF)


def run_step(scalars, arrays, latent, cells, particles, width):
    vmem = pl.BlockSpec(memory_space=pltpu.VMEM)
    smem = pl.BlockSpec(memory_space=pltpu.SMEM)
    window = cells + 2
    tile = (particles, width)
    pairs = scalars[1].shape[-1]
    return pl.pallas_call(
        step_kernel,
        in_specs=[smem] * len(scalars) + [vmem] * len(arrays),
        out_specs=[vmem] * 4,
        out_shape=[
            jax.ShapeDtypeStruct(latent.shape, BF),
            jax.ShapeDtypeStruct(latent.shape, F32),
            jax.ShapeDtypeStruct((2,) + tile, BF),
            jax.ShapeDtypeStruct((PACK_ROWS, width), BF),
        ],
        scratch_shapes=[
            pltpu.SMEM((window,), jnp.int32),
            pltpu.VMEM((window, META, particles), F32),
            pltpu.VMEM((window,) + tile, F32),
            pltpu.VMEM((window,) + tile, F32),
            pltpu.VMEM((cells,) + tile, F32),
            pltpu.VMEM((window,) + tile, F32),
            pltpu.VMEM((pairs, particles, particles), BF),
            pltpu.VMEM((pairs, particles, particles), BF),
            pltpu.VMEM((cells,) + tile, F32),
            pltpu.VMEM((cells,) + tile, F32),
            pltpu.VMEM((cells,) + tile, F32),
            pltpu.VMEM((cells,) + tile, F32),
            pltpu.VMEM((window,) + tile, F32),
            pltpu.VMEM(tile, F32),
            pltpu.VMEM(tile, BF),
            pltpu.VMEM(tile, F32),
            pltpu.VMEM(tile, BF),
            pltpu.VMEM(tile, F32),
            pltpu.VMEM((8, width), F32),
        ],
        compiler_params=pltpu.CompilerParams(vmem_limit_bytes=40 << 20),
        name="step",
    )(*scalars, *arrays)


def finish_kernel(
    core_ref,
    mine_ref,
    other_ref,
    partial_ref,
    rims_ref,
    source_w_ref,
    latent_grad_ref,
    target_w_out,
    source_w_out,
    offset_out,
    bias_out,
    edge_out_out,
    node_in_out,
    in_bias_out,
    node_out_out,
    out_bias_out,
    gain_out,
    *,
    scale,
):
    cells = partial_ref.shape[2]
    mine = mine_ref[...].astype(F32)
    other = other_ref[...].astype(F32)
    first = core_ref[0] == 0
    low = jnp.where(first, mine, other) * scale
    high = jnp.where(first, other, mine) * scale
    whole = jnp.concatenate([low, high], axis=0)
    target_w_out[...] = whole[0:128]
    source_w_out[...] = whole[128:256]
    edge_out_out[...] = whole[256:384]
    node_in_out[...] = whole[384:640]
    node_out_out[...] = whole[640:768]
    small = whole[768:776] + whole[776:784]
    offset_out[...] = small[0:2]
    bias_out[...] = small[2:3]
    in_bias_out[...] = small[3:4]
    out_bias_out[...] = small[4:5]
    gain_out[...] = small[5:6]
    latent_grad_ref[...] = partial_ref[...]
    latent_grad_ref[0, 0, cells - 1] += dot_t(rims_ref[0], source_w_ref[...])
    latent_grad_ref[0, 0, 0] += dot_t(rims_ref[1], source_w_ref[...])


def run_finish(core, mine, other, partial, rims, source_w, scale):
    width = mine.shape[-1]
    vmem = pl.BlockSpec(memory_space=pltpu.VMEM)
    smem = pl.BlockSpec(memory_space=pltpu.SMEM)
    square = jax.ShapeDtypeStruct((width, width), F32)
    row = jax.ShapeDtypeStruct((1, width), F32)
    return pl.pallas_call(
        functools.partial(finish_kernel, scale=scale),
        in_specs=[smem] + [vmem] * 5,
        out_specs=[vmem] * 11,
        out_shape=[
            jax.ShapeDtypeStruct(partial.shape, F32),
            square,
            square,
            jax.ShapeDtypeStruct((2, width), F32),
            row,
            square,
            jax.ShapeDtypeStruct((2 * width, width), F32),
            row,
            square,
            row,
            row,
        ],
        compiler_params=pltpu.CompilerParams(vmem_limit_bytes=32 << 20),
        name="finish",
    )(core, mine, other, partial, rims, source_w)


def neighbours(axis, by):
    length = lax.axis_size(axis)
    return [(i, i + by) for i in range(length) if 0 <= i + by < length]


def swap_cores(array):
    size = lax.axis_size("wide")
    return lax.ppermute(array, "wide", [(i, i ^ 1) for i in range(size)])


def exchange(array, axis, groups=None):
    return lax.all_to_all(array, axis, 0, 0, axis_index_groups=groups, tiled=True)


def spread(array, count):
    return jnp.broadcast_to(array[None], (count,) + array.shape)


def sum_everywhere(pack, core):
    width = pack.shape[-1]
    space = lax.axis_size("space")
    wide = lax.axis_size("wide")
    fellows = [list(range(start, wide, 2)) for start in range(2)]
    halves = pack.reshape(2, -1, width)
    mine = jnp.where(core == 0, halves[0], halves[1])
    sent = jnp.where(core == 0, halves[1], halves[0])
    half = mine.astype(F32) + swap_cores(sent).astype(F32)
    parts = half.astype(BF).reshape(space, -1, width)
    part = jnp.sum(exchange(parts, "space").astype(F32), axis=0).astype(BF)
    others = exchange(spread(part, wide // 2), "wide", fellows)
    part = jnp.sum(others.astype(F32), axis=0).astype(BF)
    return exchange(spread(part, space), "space").reshape(-1, width)


def on_device(
    latent,
    coords,
    cell_counts,
    pair_target,
    pair_source,
    pair_count,
    edge_target_w,
    edge_source_w,
    edge_offset,
    edge_bias,
    edge_out,
    node_in,
    node_in_bias,
    node_out,
    node_out_bias,
    norm_gain,
    cotangent,
):
    cells, particles, width = latent.shape[2:]
    core = lax.rem(lax.axis_index("wide"), 2)
    live = (
        jnp.arange(particles, dtype=jnp.int32)[None, :] < cell_counts[0, 0][:, None]
    ).astype(BF)
    meta = jnp.concatenate(
        [coords[0, 0], live[:, None, :], jnp.zeros((cells, META - 3, particles), BF)], axis=1
    )
    last = jnp.concatenate([latent[0, 0, cells - 1], meta[cells - 1]], axis=0)
    initial = jnp.concatenate([latent[0, 0, 0], meta[0]], axis=0)
    before = lax.ppermute(last, "space", neighbours("space", 1))
    after = lax.ppermute(initial, "space", neighbours("space", -1))
    new_rows, partial, rims, pack = run_step(
        (cell_counts, pair_target, pair_source, pair_count),
        (
            latent,
            meta,
            before,
            after,
            edge_target_w,
            edge_source_w,
            edge_offset,
            edge_bias[None, :],
            edge_out,
            node_in,
            node_in_bias[None, :],
            node_out,
            node_out_bias[None, :],
            norm_gain[None, :],
            cotangent,
        ),
        latent,
        cells,
        particles,
        width,
    )
    from_next = lax.ppermute(rims[0], "space", neighbours("space", -1))
    from_prev = lax.ppermute(rims[1], "space", neighbours("space", 1))
    mine = sum_everywhere(pack, core)
    other = swap_cores(mine)
    scale = 1.0 / math.sqrt(lax.axis_size("space") * lax.axis_size("wide") * cells * particles)
    rims_in = jnp.stack([from_next, from_prev])
    outs = run_finish(
        core.astype(jnp.int32)[None], mine, other, partial, rims_in, edge_source_w, scale
    )
    (latent_grad, target_w, source_w, offset, bias, out_w, in_w, in_bias, node_w, out_bias, gain) = outs
    return (
        new_rows,
        latent_grad,
        target_w,
        source_w,
        offset,
        bias[0],
        out_w,
        in_w,
        in_bias[0],
        node_w,
        out_bias[0],
        gain[0],
    )


def solution(mesh):
    cell = P("wide", "space", None, None, None)
    table = P("wide", "space", None)
    return jax.shard_map(
        on_device,
        mesh=mesh,
        in_specs=(cell, cell, table, table, table, P("wide", "space")) + (P(),) * 10 + (cell,),
        out_specs=(cell, cell) + (P(),) * 10,
        check_vma=False,
    )
```

time: 795 us -> 140 us (0.18)
  waiting for transfers between devices: 274 us -> 7.03 us
  other arithmetic: 190 us -> 0.97 us
  loops' own time: 142 us -> 0 us
  blocking collectives: 112 us -> 56.6 us
  Pallas kernels: 0 us -> 39.4 us
  local copies, waits for them, and re-layouts: 33.6 us -> 7.92 us
  between operations: 14.6 us -> 1.5 us
    psum x1 -> x0, waiting for transfers between devices: 269 us -> none  [on_device(): lax.psum((grad_target_w, grad_source_w, grad_offset, grad_bias, grad_edge...]
    reduce_sum x29 -> x2, other arithmetic: 180 us -> 0.06 us  [the longest x1 0.03 us: sum_everywhere(): part = jnp.sum(exchange(parts, 'space').astype(F32), axis=0).astype(BF)]
    another operation x2 -> x0, loops' own time: 142 us -> none  [the longest x1 71.3 us: edge_backward(): return lax.fori_loop(0, slot_stop, visit, start)]
    psum x1 -> x0, blocking collectives: 112 us -> none  [on_device(): lax.psum((grad_target_w, grad_source_w, grad_offset, grad_bias, grad_edge...]
    all_to_all x0 -> x2, blocking collectives: none -> 56.6 us  [exchange(): lax.all_to_all(array, axis, 0, 0, axis_index_groups=groups, tiled=True)]
    pallas_call x0 -> x2, Pallas kernels: none -> 39.4 us  [the longest x1 38.5 us: run_step(): pl.pallas_call(step_kernel, in_specs=[smem] * len(scalars) + [vmem] * len...]
    dynamic_slice x48 -> x0, local copies, waits for them, and re-layouts: 28.2 us -> none  [the longest x24 14.1 us: visit(): source = sources[slot_index]]
    ppermute x8 -> x6, starting transfers between devices: 18.7 us -> 22.6 us  [the longest x2 12.1 us: swap_cores(): return lax.ppermute(array, 'wide', [(i, i ^ 1) for i in range(size)])]
  transfers between devices with their start and end apart: 9 -> 7, of which waited for: 3 -> 4; matrix products, arithmetic and copies ran while one was open for 1% -> 0% of each run, Pallas kernels for 0% -> 0%
where the time goes in v1:
time: 140 us
  blocking collectives  56.6 us (40%)
  Pallas kernels  39.4 us (28%)
  starting transfers between devices  26.3 us (19%)
  local copies, waits for them, and re-layouts  7.92 us (6%)
  waiting for transfers between devices  7.03 us (5%)
  between operations  1.5 us (1%)
    all_to_all x2, blocking collectives, exchange(): lax.all_to_all(array, axis, 0, 0, axis_index_groups=groups, tiled=True)  56.6 us
    pallas_call x1, Pallas kernels, run_step(): pl.pallas_call(step_kernel, in_specs=[smem] * len(scalars) + [vmem] * len...  38.5 us
    ppermute x2, starting transfers between devices, swap_cores(): return lax.ppermute(array, 'wide', [(i, i ^ 1) for i in range(size)])  12.1 us
    unnamed x30, local copies, waits for them, and re-layouts  6.21 us
    ppermute x1, starting transfers between devices, on_device(): from_prev = lax.ppermute(rims[1], 'space', neighbours('space', 1))  3.99 us
    ppermute x1, starting transfers between devices, on_device(): before = lax.ppermute(last, 'space', neighbours('space', 1))  3.95 us
    all_to_all x1, starting transfers between devices, exchange(): lax.all_to_all(array, axis, 0, 0, axis_index_groups=groups, tiled=True)  3.71 us
  transfers between devices with their start and end apart: 7, of which 4 were waited for; matrix products, arithmetic and copies ran while one was open for 0% of the time, Pallas kernels for 0%

profile of v1, /device:TPU:1, one launch (start us, length us, event | category | flops | bytes accessed | tf_op | source)
XLA Modules:
  0.0 139.7 jit_solution(15859864482760496035)
XLA Ops:
  0.6 0.0 copy-start.7
  0.7 0.0 copy-start.3
  0.7 0.6 copy-done.7
  1.3 0.1 compare_convert_fusion
  1.4 0.1 pad.8.clone
  1.5 0.8 maximum_maximum_fusion.meta_ref
  2.2 0.0 copy-start
  2.2 0.0 copy-start.2
  2.2 0.8 slice_bitcast_fusion.2
  3.1 3.9 %collective-permute-start = (bf16[144,128]{1,0:T(8,128)(2,1)S(1)}, bf16[144,128]{1,0:T(8,128)(2,1)S(1)}, u32[]{:S(2)}, u32[]{:S(2)}) collective-permute-start(bf16[144,128]{1,0:T(8,128)(2,1)S(1)} %pad_maximum_fusion.1), channel_id=1, source_target_pairs={{0,32},{32,64},{64,96},{96,128},{128,160},{160,192},{192,224},{224... | collective-permute-start | bytes 110600 | tf_op jit(solution)/shard_map/ppermute | solution.py:515
  7.0 0.0 copy-start.1
  7.0 1.3 collective-permute-start.1
  9.0 0.0 collective-permute-done.before_ref
  9.0 2.7 %collective-permute-done.1.after_ref = bf16[144,128]{1,0:T(8,128)(2,1)S(1)} collective-permute-done((bf16[144,128]{1,0:T(8,128)(2,1)S(1)}, bf16[144,128]{1,0:T(8,128)(2,1)S(1)}, u32[]{:S(2)}, u32[]{:S(2)}) %collective-permute-start.1) | collective-permute-done | bytes 36896 | tf_op jit(solution)/shard_map/ppermute | solution.py:516
  11.7 0.0 copy-start.10
  11.8 0.0 copy-start.9
  11.8 0.0 copy-done.3
  11.8 0.0 copy-done
  11.8 0.0 copy-done.2
  11.8 0.0 copy-done.1
  11.8 0.6 copy-done.10
  12.4 0.0 copy-done.8
  12.4 0.0 copy-done.9
  12.4 0.0 copy-start.4
  12.4 0.8 copy-done.4
  13.2 0.0 copy-start.5
  13.2 0.8 copy-done.5
  14.0 0.0 copy-start.6
  14.0 0.8 copy-done.6
  14.7 0.7 copy-done.11
  15.4 0.7 copy-done.12
  16.0 0.7 copy-done.13
  16.7 0.7 copy-done.14
  17.3 38.5 %step.1 = (bf16[1,1,4,128,128]{4,3,2,1,0:T(8,128)(2,1)}, f32[1,1,4,128,128]{4,3,2,1,0:T(8,128)S(1)}, bf16[2,128,128]{2,1,0:T(8,128)(2,1)S(1)}, bf16[800,128]{1,0:T(8,128)(2,1)S(1)}) custom-call(s32[1,1,4]{2,1,0:T(1,128)S(1)} %copy-done.7, s32[1,1,12]{2,1,0:T(1,128)S(1)} %copy-done.9, s32[1,1,12]{2,1,0:T(1,128)S(1)} %copy-done.10, ...), custom_call_target="tpu_custom_call" | custom-call | tf_op jit(solution)/shard_map/step/pallas_call | solution.py:344
  55.8 6.0 %collective-permute-start.2 = (bf16[400,128]{1,0:T(8,128)(2,1)S(1)}, bf16[400,128]{1,0:T(8,128)(2,1)S(1)}, u32[]{:S(2)}, u32[]{:S(2)}) collective-permute-start(bf16[400,128]{1,0:T(8,128)(2,1)S(1)} %broadcast_select_fusion), channel_id=1, source_target_pairs={{0,1},{1,0},{2,3},{3,2},{4,5},{5,4},{6,7},{7,6},{8,9},{9,8},{10,11... | collective-permute-start | bytes 307208 | tf_op jit(solution)/shard_map/ppermute | solution.py:459
  61.9 0.9 collective-permute-done.2
  62.9 25.0 %all_to_all.15 = bf16[16,25,128]{2,1,0:T(8,128)(2,1)S(1)} all-to-all(bf16[16,25,128]{2,1,0:T(8,128)(2,1)S(1)} %reshape.78), channel_id=1, replica_groups=mesh['space'=16,'wide'=32] {'space'}, dimensions={0} | all-to-all | bytes 204800 | tf_op jit(solution)/shard_map/all_to_all | solution.py:463
  88.0 31.5 %all_to_all.16 = bf16[16,25,128]{2,1,0:T(8,128)(2,1)S(1)} all-to-all(bf16[16,25,128]{2,1,0:T(8,128)(2,1)S(1)} %broadcast_in_dim.38), channel_id=1, replica_groups={{0,2,4,6,8,10,12,14,16,18,20,22,24,26,28,30},{1,3,5,7,9,11,13,15,17,19,..., dimensions={0} | all-to-all | bytes 204800 | tf_op jit(solution)/shard_map/all_to_all | solution.py:463
  119.5 0.7 broadcast_in_dim.39
  120.2 3.7 %all-to-all-start.2 = ((bf16[16,25,128]{2,1,0:T(8,128)(2,1)}), bf16[16,25,128]{2,1,0:T(8,128)(2,1)S(1)}, u32[]{:S(2)}, u32[]{:S(2)}) async-start(bf16[16,25,128]{2,1,0:T(8,128)(2,1)} %broadcast_in_dim.39), calls=%async_computation.2 | async-start | bytes 262144 | tf_op jit(solution)/shard_map/all_to_all | solution.py:463
  123.9 1.3 collective-permute-start.4
  125.2 4.0 %collective-permute-start.5 = (bf16[128,128]{1,0:T(8,128)(2,1)S(1)}, bf16[128,128]{1,0:T(8,128)(2,1)S(1)}, u32[]{:S(2)}, u32[]{:S(2)}) collective-permute-start(bf16[128,128]{1,0:T(8,128)(2,1)S(1)} %get-tuple-element.45), channel_id=1, source_target_pairs={{0,32},{32,64},{64,96},{96,128},{128,160},{160,192},{192,224},{224... | collective-permute-start | bytes 98312 | tf_op jit(solution)/shard_map/ppermute | solution.py:542
  129.2 2.5 %all-to-all-done.2 = bf16[16,25,128]{2,1,0:T(8,128)(2,1)S(1)} async-done(((bf16[16,25,128]{2,1,0:T(8,128)(2,1)}), bf16[16,25,128]{2,1,0:T(8,128)(2,1)S(1)}, u32[]{:S(2)}, u32[]{:S(2)}) %all-to-all-start.2) | async-done | bytes 102432 | tf_op jit(solution)/shard_map/all_to_all | solution.py:463
  131.8 6.1 %collective-permute-start.3 = (bf16[400,128]{1,0:T(8,128)(2,1)S(1)}, bf16[400,128]{1,0:T(8,128)(2,1)S(1)}, u32[]{:S(2)}, u32[]{:S(2)}) collective-permute-start(bf16[400,128]{1,0:T(8,128)(2,1)S(1)} %reshape.79.mine_ref), channel_id=1, source_target_pairs={{0,1},{1,0},{2,3},{3,2},{4,5},{5,4},{6,7},{7,6},{8,9},{9,8},{10,11... | collective-permute-start | bytes 307208 | tf_op jit(solution)/shard_map/ppermute | solution.py:459
  137.8 0.0 collective-permute-done.4
  137.8 0.0 collective-permute-done.5
  137.9 0.9 collective-permute-done.3.other_ref
  138.8 0.9 finish.1
  (18 shorter events, 0.3 us)
Async XLA Ops:
  0.6 0.7 copy-start.7
  0.7 11.1 %copy-start.3 = (bf16[256,128]{1,0:T(8,128)(2,1)S(1)}, bf16[256,128]{1,0:T(8,128)(2,1)}, u32[]{:S(2)}) copy-start(bf16[256,128]{1,0:T(8,128)(2,1)} %node_in_ref.1) | copy-start | bytes 196612
  2.2 9.5 %copy-start = (bf16[1,1,4,128,128]{4,3,2,1,0:T(8,128)(2,1)S(1)}, bf16[1,1,4,128,128]{4,3,2,1,0:T(8,128)(2,1)}, u32[]{:S(2)}) copy-start(bf16[1,1,4,128,128]{4,3,2,1,0:T(8,128)(2,1)} %latent_ref.1) | copy-start | bytes 393220
  2.2 9.6 %copy-start.2 = (bf16[1,1,4,128,128]{4,3,2,1,0:T(8,128)(2,1)S(1)}, bf16[1,1,4,128,128]{4,3,2,1,0:T(8,128)(2,1)}, u32[]{:S(2)}) copy-start(bf16[1,1,4,128,128]{4,3,2,1,0:T(8,128)(2,1)} %cotangent_ref.1) | copy-start | bytes 393220
  3.1 5.9 %collective-permute-start = (bf16[144,128]{1,0:T(8,128)(2,1)S(1)}, bf16[144,128]{1,0:T(8,128)(2,1)S(1)}, u32[]{:S(2)}, u32[]{:S(2)}) collective-permute-start(bf16[144,128]{1,0:T(8,128)(2,1)S(1)} %pad_maximum_fusion.1), channel_id=1, source_target_pairs={{0,32},{32,64},{64,96},{96,128},{128,160},{160,192},{192,224},{224... | collective-permute-start | bytes 110600 | tf_op jit(solution)/shard_map/ppermute | solution.py:515
  7.0 4.8 %copy-start.1 = (bf16[128,128]{1,0:T(8,128)(2,1)S(1)}, bf16[128,128]{1,0:T(8,128)(2,1)}, u32[]{:S(2)}) copy-start(bf16[128,128]{1,0:T(8,128)(2,1)} %source_w_ref.3) | copy-start | bytes 98308
  7.0 4.7 %collective-permute-start.1 = (bf16[144,128]{1,0:T(8,128)(2,1)S(1)}, bf16[144,128]{1,0:T(8,128)(2,1)S(1)}, u32[]{:S(2)}, u32[]{:S(2)}) collective-permute-start(bf16[144,128]{1,0:T(8,128)(2,1)S(1)} %pad_maximum_fusion.2), channel_id=1, source_target_pairs={{32,0},{64,32},{96,64},{128,96},{160,128},{192,160},{224,192},{256... | collective-permute-start | bytes 110600 | tf_op jit(solution)/shard_map/ppermute | solution.py:516
  11.7 0.7 copy-start.10
  11.7 0.7 copy-start.8
  11.8 0.7 copy-start.9
  12.4 0.8 copy-start.4
  13.2 0.8 copy-start.5
  14.0 0.8 copy-start.6
  14.7 0.7 copy-start.11
  15.4 0.7 copy-start.12
  16.0 0.7 copy-start.13
  16.7 0.7 copy-start.14
  55.8 6.9 %collective-permute-start.2 = (bf16[400,128]{1,0:T(8,128)(2,1)S(1)}, bf16[400,128]{1,0:T(8,128)(2,1)S(1)}, u32[]{:S(2)}, u32[]{:S(2)}) collective-permute-start(bf16[400,128]{1,0:T(8,128)(2,1)S(1)} %broadcast_select_fusion), channel_id=1, source_target_pairs={{0,1},{1,0},{2,3},{3,2},{4,5},{5,4},{6,7},{7,6},{8,9},{9,8},{10,11... | collective-permute-start | bytes 307208 | tf_op jit(solution)/shard_map/ppermute | solution.py:459
  120.2 11.5 %all-to-all-start.2 = ((bf16[16,25,128]{2,1,0:T(8,128)(2,1)}), bf16[16,25,128]{2,1,0:T(8,128)(2,1)S(1)}, u32[]{:S(2)}, u32[]{:S(2)}) async-start(bf16[16,25,128]{2,1,0:T(8,128)(2,1)} %broadcast_in_dim.39), calls=%async_computation.2 | async-start | bytes 262144 | tf_op jit(solution)/shard_map/all_to_all | solution.py:463
  123.9 13.9 %collective-permute-start.4 = (bf16[128,128]{1,0:T(8,128)(2,1)S(1)}, bf16[128,128]{1,0:T(8,128)(2,1)S(1)}, u32[]{:S(2)}, u32[]{:S(2)}) collective-permute-start(bf16[128,128]{1,0:T(8,128)(2,1)S(1)} %get-tuple-element.44), channel_id=1, source_target_pairs={{32,0},{64,32},{96,64},{128,96},{160,128},{192,160},{224,192},{256... | collective-permute-start | bytes 98312 | tf_op jit(solution)/shard_map/ppermute | solution.py:541
  125.2 12.6 %collective-permute-start.5 = (bf16[128,128]{1,0:T(8,128)(2,1)S(1)}, bf16[128,128]{1,0:T(8,128)(2,1)S(1)}, u32[]{:S(2)}, u32[]{:S(2)}) collective-permute-start(bf16[128,128]{1,0:T(8,128)(2,1)S(1)} %get-tuple-element.45), channel_id=1, source_target_pairs={{0,32},{32,64},{64,96},{96,128},{128,160},{160,192},{192,224},{224... | collective-permute-start | bytes 98312 | tf_op jit(solution)/shard_map/ppermute | solution.py:542
  131.8 7.0 %collective-permute-start.3 = (bf16[400,128]{1,0:T(8,128)(2,1)S(1)}, bf16[400,128]{1,0:T(8,128)(2,1)S(1)}, u32[]{:S(2)}, u32[]{:S(2)}) collective-permute-start(bf16[400,128]{1,0:T(8,128)(2,1)S(1)} %reshape.79.mine_ref), channel_id=1, source_target_pairs={{0,1},{1,0},{2,3},{3,2},{4,5},{5,4},{6,7},{7,6},{8,9},{9,8},{10,11... | collective-permute-start | bytes 307208 | tf_op jit(solution)/shard_map/ppermute | solution.py:459

commit v2 on v1

--- a/solution.py
+++ b/solution.py
@@ -12,6 +12,8 @@
 F32 = jnp.float32
 META = 16
 GRAIN = 16
+STEP = 16
+ROWS = 64
 PACK_ROWS = 800
 
 
@@ -31,8 +33,8 @@
     return 0.5 * (1.0 + jnp.tanh(0.5 * v))
 
 
-def blocks(count):
-    return lax.div(count + (GRAIN - 1), GRAIN)
+def blocks(count, rows):
+    return lax.div(count + (rows - 1), rows)
 
 
 def column_sum(values):
@@ -82,41 +84,60 @@
     b_half_ref,
     pair_sum_ref,
     shift_ref,
+    order_ref,
+    rows_ref,
+    cotangent_rows_ref,
+    bounds_ref,
+    bounds_smem,
+    bounds_sem,
 ):
     cells, particles, width = latent_ref.shape[2:]
     rows = cells * particles
     offset_x = offset_ref[0:1, :]
     offset_y = offset_ref[1:2, :]
 
-    for cell in range(cells):
-        live_ref[cell + 1] = counts_ref[0, 0, cell]
-        place_ref[cell + 1] = meta_ref[cell].astype(F32)
-    place_ref[0] = before_ref[particles:, :].astype(F32)
-    place_ref[cells + 1] = after_ref[particles:, :].astype(F32)
-    live_ref[0] = jnp.sum(place_ref[0, 2:3, :]).astype(jnp.int32)
-    live_ref[cells + 1] = jnp.sum(place_ref[cells + 1, 2:3, :]).astype(jnp.int32)
-
+    sub = lax.broadcasted_iota(jnp.int32, (particles, particles), 0)
+    lane = lax.broadcasted_iota(jnp.int32, (particles, particles), 1)
     pick = lax.broadcasted_iota(jnp.int32, (META, width), 0)
     pick_x = jnp.where(pick == 0, 1.0, 0.0).astype(BF)
     pick_y = jnp.where(pick == 1, 1.0, 0.0).astype(BF)
+    pick_key = jnp.where(pick == 3, 1.0, 0.0).astype(BF)
     for slot in range(cells + 2):
         if slot == 0:
             rows_in = before_ref[:particles, :]
+            place = before_ref[particles:, :].astype(F32)
+            live_ref[slot] = jnp.sum(place[2:3, :]).astype(jnp.int32)
         elif slot == cells + 1:
             rows_in = after_ref[:particles, :]
+            place = after_ref[particles:, :].astype(F32)
+            live_ref[slot] = jnp.sum(place[2:3, :]).astype(jnp.int32)
         else:
             rows_in = latent_ref[0, 0, slot - 1]
-        place = place_ref[slot].astype(BF)
+            place = meta_ref[slot - 1].astype(F32)
+            live_ref[slot] = counts_ref[0, 0, slot - 1]
+        key = jnp.where(place[2:3, :] > 0.5, place[0:1, :], 2.0)
+        place = jnp.where(pick == 3, key, place).astype(BF)
+        keys = t_dot(place, pick_key)
+        ahead = (keys < key) | ((keys == key) & (sub < lane))
+        rank = column_sum(jnp.where(ahead, 1.0, 0.0))
+        order = jnp.where(sub.astype(F32) == rank, 1.0, 0.0).astype(BF)
+        order_ref[slot] = order
+        place = dot_t(place, order)
+        place_ref[slot] = place
+        place = place.astype(BF)
         x = t_dot(place, pick_x)
         y = t_dot(place, pick_y)
         x_ref[slot] = x
         y_ref[slot] = y
         moved = x * offset_x + (y - 0.5) * offset_y
+        rows_in = dot(order, rows_in).astype(BF)
+        rows_ref[slot] = rows_in
         proj_source = dot(rows_in, source_w_ref[...]).astype(BF).astype(F32)
         b_base_ref[slot] = 0.5 * (proj_source - moved)
         if 0 < slot < cells + 1:
             proj_target = (dot(rows_in, target_w_ref[...]) + bias_ref[...]).astype(BF)
             a_base_ref[slot - 1] = 0.5 * (proj_target.astype(F32) + moved)
+            cotangent_rows_ref[slot - 1] = dot(order, cotangent_ref[0, 0, slot - 1]).astype(BF)
 
     aggregate_ref[...] = jnp.zeros_like(aggregate_ref)
     slope_ref[...] = jnp.zeros_like(slope_ref)
@@ -125,8 +146,6 @@
     shift_ref[...] = jnp.zeros_like(shift_ref)
 
     row_of = lax.broadcasted_iota(jnp.int32, (GRAIN, width), 0)
-    sub = lax.broadcasted_iota(jnp.int32, (particles, particles), 0)
-    lane = lax.broadcasted_iota(jnp.int32, (particles, particles), 1)
     listed = listed_ref[0, 0]
 
     def pair_of(slot):
@@ -144,9 +163,49 @@
         a_half_ref[...] = a.astype(BF)
         b_half_ref[...] = b.astype(BF)
 
-    def over_sizes(count, visit):
-        for size in range(2 * GRAIN, particles + 1, GRAIN):
-            pl.when(blocks(count) == size // GRAIN)(functools.partial(visit, size))
+    def bound_pair(slot, _):
+        target, source, off, _, _ = pair_of(slot)
+        live_target = live_ref[target + 1]
+        live_source = live_ref[source]
+
+        def counted(hit):
+            return column_sum(jnp.where(hit, 1.0, 0.0)).astype(jnp.int32)
+
+        x_target, row_target = x_ref[target + 1], place_ref[target + 1, 0:1, :]
+        x_source, row_source = x_ref[source], place_ref[source, 0:1, :]
+        zero = jnp.zeros((1, particles), jnp.int32)
+        source_at_most = counted((x_source <= row_target) & (sub < live_source))
+        source_below = counted((x_source < row_target) & (sub < live_source))
+        target_at_most = counted((x_target <= row_source) & (sub < live_target))
+        target_below = counted((x_target < row_source) & (sub < live_target))
+        bounds_ref[slot] = jnp.concatenate(
+            [
+                jnp.where(off > 0.5, source_at_most, zero),
+                jnp.where(off < -0.5, source_below, zero + live_source),
+                jnp.where(off < -0.5, target_at_most, zero),
+                jnp.where(off > 0.5, target_below, zero + live_target),
+                jnp.zeros((4, particles), jnp.int32),
+            ],
+            axis=0,
+        )
+        return 0
+
+    lax.fori_loop(0, listed, bound_pair, 0)
+    bounds_copy = pltpu.make_async_copy(bounds_ref, bounds_smem, bounds_sem)
+    bounds_copy.start()
+    bounds_copy.wait()
+
+    def over_range(slot, which, first, live, visit):
+        last = jnp.minimum(first + (ROWS - 1), live - 1)
+        start = lax.div(bounds_smem[slot, which, first], STEP)
+        most = particles // STEP
+        size = jnp.clip(blocks(bounds_smem[slot, which + 1, last], STEP) - start, 0, most)
+        lax.switch(
+            size,
+            [lambda at: None]
+            + [functools.partial(visit, STEP * count) for count in range(1, most + 1)],
+            jnp.clip(start, 0, most - size) * STEP,
+        )
 
     def forward_pair(slot, _):
         target, source, off, alpha, beta = pair_of(slot)
@@ -173,30 +232,34 @@
             aggregate_ref[target] += a_ref[...] * weight_sum + linear[:, :width]
             pair_sum_ref[...] = weight_sum
 
-            def visit(size):
-                def block(index, _):
-                    first = pl.multiple_of(index * GRAIN, GRAIN)
-                    here = pl.ds(first, GRAIN)
-                    weights = weight_ref[slot, here, :]
-                    b = b_half_ref[0:size, :]
-                    total = jnp.zeros((GRAIN, 2 * width), F32)
-                    for r in range(GRAIN):
-                        a = a_ref[pl.ds(first + r, 1), :].astype(BF)
-                        u = jnp.broadcast_to(a, (size, width)) + b
-                        t = jnp.tanh(u)
-                        bent = u * t
-                        steep = t + u * (1.0 - t * t)
-                        one = jnp.where(row_of == r, weights, jnp.zeros_like(weights))
-                        total = total + dot(
-                            one[:, :size], jnp.concatenate([bent, steep], axis=1)
-                        )
-                    aggregate_ref[target, here, :] += total[:, :width]
-                    pair_sum_ref[here, :] += total[:, width:]
-                    return 0
-
-                lax.fori_loop(0, blocks(live_target), block, 0)
-
-            over_sizes(live_source, visit)
+            def block(index, _):
+                first = pl.multiple_of(index * ROWS, ROWS)
+
+                def visit(size, at):
+                    at = pl.multiple_of(at, STEP)
+                    b = b_half_ref[pl.ds(at, size), :]
+                    for group in range(0, ROWS, GRAIN):
+                        here = pl.ds(first + group, GRAIN)
+                        weights = weight_ref[slot, here, :].astype(F32)
+                        weights = pltpu.roll(weights, particles - at, axis=1).astype(BF)
+                        total = jnp.zeros((GRAIN, 2 * width), F32)
+                        for r in range(GRAIN):
+                            a = a_ref[pl.ds(first + group + r, 1), :].astype(BF)
+                            u = jnp.broadcast_to(a, (size, width)) + b
+                            t = jnp.tanh(u)
+                            bent = u * t
+                            steep = t + u * (1.0 - t * t)
+                            one = jnp.where(row_of == r, weights, jnp.zeros_like(weights))
+                            total = total + dot(
+                                one[:, :size], jnp.concatenate([bent, steep], axis=1)
+                            )
+                        aggregate_ref[target, here, :] += total[:, :width]
+                        pair_sum_ref[here, :] += total[:, width:]
+
+                over_range(slot, 0, first, live_target, visit)
+                return 0
+
+            lax.fori_loop(0, blocks(live_target, ROWS), block, 0)
             slope_ref[target] += pair_sum_ref[...]
             slope_shift_ref[target] += alpha * pair_sum_ref[...]
 
@@ -204,7 +267,7 @@
 
     lax.fori_loop(0, listed, forward_pair, 0)
 
-    latent = latent_ref[0, 0].reshape(rows, width)
+    latent = rows_ref[1 : cells + 1].reshape(rows, width)
     agg_b = aggregate_ref[...].reshape(rows, width).astype(BF)
     message = dot(agg_b, edge_out_ref[...]).astype(BF)
     hidden_pre = (
@@ -220,9 +283,11 @@
     normed = centred * inverse
     gain = gain_ref[...]
     new_rows = (latent.astype(F32) + normed * gain).astype(BF)
-    new_latent_ref[0, 0] = new_rows.reshape(cells, particles, width)
-
-    cotangent = cotangent_ref[0, 0].reshape(rows, width).astype(F32)
+    for cell in range(cells):
+        there = new_rows[cell * particles : (cell + 1) * particles]
+        new_latent_ref[0, 0, cell] = t_dot(order_ref[cell + 1], there).astype(BF)
+
+    cotangent = cotangent_rows_ref[...].reshape(rows, width).astype(F32)
     gain_sum = column_sum(cotangent * normed)
     scaled = cotangent * gain
     grad_pre = inverse * (
@@ -245,7 +310,7 @@
     upstream = dot_t(grad_message, edge_out_ref[...])
     upstream_ref[...] = upstream.reshape(cells, particles, width)
     grad_rows = cotangent + dot_t(grad_hidden_b, node_in_ref[:width, :])
-    latent_grad_ref[0, 0] = grad_rows.reshape(cells, particles, width)
+    aggregate_ref[...] = grad_rows.reshape(cells, particles, width)
 
     def backward_pair(slot, _):
         target, source, _, alpha, beta = pair_of(slot)
@@ -257,31 +322,36 @@
             set_pair(target, source, alpha, beta)
             pair_sum_ref[...] = dot(weight_t_ref[slot], upstream_ref[target].astype(BF))
 
-            def visit(size):
-                def block(index, _):
-                    first = pl.multiple_of(index * GRAIN, GRAIN)
-                    here = pl.ds(first, GRAIN)
-                    weights = weight_t_ref[slot, here, :][:, :size]
-                    a = a_half_ref[0:size, :]
-                    up = upstream_ref[target, 0:size, :].astype(BF)
-
-                    def steep(r):
-                        b = b_ref[pl.ds(first + r, 1), :].astype(BF)
+            def block(index, _):
+                first = pl.multiple_of(index * ROWS, ROWS)
+
+                def visit(size, at):
+                    at = pl.multiple_of(at, STEP)
+                    a = a_half_ref[pl.ds(at, size), :]
+                    up = upstream_ref[target, pl.ds(at, size), :].astype(BF)
+
+                    def steep(row):
+                        b = b_ref[pl.ds(first + row, 1), :].astype(BF)
                         u = jnp.broadcast_to(b, (size, width)) + a
                         t = jnp.tanh(u)
                         return up * (t + u * (1.0 - t * t))
 
-                    total = jnp.zeros((GRAIN, width), F32)
-                    for r in range(0, GRAIN, 2):
-                        both = dot(weights, jnp.concatenate([steep(r), steep(r + 1)], axis=1))
-                        total = jnp.where(row_of == r, both[:, :width], total)
-                        total = jnp.where(row_of == r + 1, both[:, width:], total)
-                    pair_sum_ref[here, :] += total
-                    return 0
-
-                lax.fori_loop(0, blocks(live_source), block, 0)
-
-            over_sizes(live_target, visit)
+                    for group in range(0, ROWS, GRAIN):
+                        here = pl.ds(first + group, GRAIN)
+                        weights = weight_t_ref[slot, here, :].astype(F32)
+                        weights = pltpu.roll(weights, particles - at, axis=1).astype(BF)
+                        total = jnp.zeros((GRAIN, width), F32)
+                        for r in range(0, GRAIN, 2):
+                            pair = jnp.concatenate([steep(group + r), steep(group + r + 1)], axis=1)
+                            both = dot(weights[:, :size], pair)
+                            total = jnp.where(row_of == r, both[:, :width], total)
+                            total = jnp.where(row_of == r + 1, both[:, width:], total)
+                        pair_sum_ref[here, :] += total
+
+                over_range(slot, 2, first, live_source, visit)
+                return 0
+
+            lax.fori_loop(0, blocks(live_source, ROWS), block, 0)
             grads = 0.5 * pair_sum_ref[...]
             source_grad_ref[source] += grads
             shift_ref[...] += beta * jnp.sum(grads.reshape(particles // 8, 8, width), axis=0)
@@ -296,17 +366,23 @@
     source_grad = source_grad_ref[...].reshape(rows + 2 * particles, width)
     source_b = source_grad.astype(BF)
     own_b = source_b[particles : particles + rows]
-    rim_grad_ref[0] = source_b[:particles]
-    rim_grad_ref[1] = source_b[particles + rows :]
-    latent = latent_ref[0, 0].reshape(rows, width)
+    rim_grad_ref[0] = t_dot(order_ref[0], source_b[:particles]).astype(BF)
+    rim_grad_ref[1] = t_dot(order_ref[cells + 1], source_b[particles + rows :]).astype(BF)
+    latent = rows_ref[1 : cells + 1].reshape(rows, width)
     pack_ref[0:128, :] = t_dot(latent, target_b).astype(BF)
     pack_ref[128:256, :] = (
         t_dot(latent, own_b)
-        + t_dot(before_ref[:particles, :], source_b[:particles])
-        + t_dot(after_ref[:particles, :], source_b[particles + rows :])
+        + t_dot(rows_ref[0], source_b[:particles])
+        + t_dot(rows_ref[cells + 1], source_b[particles + rows :])
     ).astype(BF)
     more = dot_t(target_b, target_w_ref[...]) + dot_t(own_b, source_w_ref[...])
-    latent_grad_ref[0, 0] += more.reshape(cells, particles, width)
+    grad_rows = aggregate_ref[...].reshape(rows, width) + more
+    for cell in range(cells):
+        there = grad_rows[cell * particles : (cell + 1) * particles]
+        coarse = there.astype(BF)
+        fine = (there - coarse.astype(F32)).astype(BF)
+        both = t_dot(order_ref[cell + 1], jnp.concatenate([coarse, fine], axis=1))
+        latent_grad_ref[0, 0, cell] = both[:, :width] + both[:, width:]
     x_target = x_ref[1 : cells + 1].reshape(rows, width)
     y_target = y_ref[1 : cells + 1].reshape(rows, width)
     x_source = x_ref[...].reshape(rows + 2 * particles, width)
@@ -335,22 +411,27 @@
     pack_ref[784:800, :] = jnp.zeros((16, width), BF)
 
 
+def whole(array):
+    return pl.BlockSpec(array.shape, lambda step: (0,) * len(array.shape))
+
+
 def run_step(scalars, arrays, latent, cells, particles, width):
-    vmem = pl.BlockSpec(memory_space=pltpu.VMEM)
     smem = pl.BlockSpec(memory_space=pltpu.SMEM)
     window = cells + 2
     tile = (particles, width)
     pairs = scalars[1].shape[-1]
+    outs = [
+        jax.ShapeDtypeStruct(latent.shape, BF),
+        jax.ShapeDtypeStruct(latent.shape, F32),
+        jax.ShapeDtypeStruct((2,) + tile, BF),
+        jax.ShapeDtypeStruct((PACK_ROWS, width), BF),
+    ]
     return pl.pallas_call(
         step_kernel,
-        in_specs=[smem] * len(scalars) + [vmem] * len(arrays),
-        out_specs=[vmem] * 4,
-        out_shape=[
-            jax.ShapeDtypeStruct(latent.shape, BF),
-            jax.ShapeDtypeStruct(latent.shape, F32),
-            jax.ShapeDtypeStruct((2,) + tile, BF),
-            jax.ShapeDtypeStruct((PACK_ROWS, width), BF),
-        ],
+        grid=(1,),
+        in_specs=[smem] * len(scalars) + [whole(array) for array in arrays],
+        out_specs=[whole(array) for array in outs],
+        out_shape=outs,
         scratch_shapes=[
             pltpu.SMEM((window,), jnp.int32),
             pltpu.VMEM((window, META, particles), F32),
@@ -371,8 +452,14 @@
             pltpu.VMEM(tile, BF),
             pltpu.VMEM(tile, F32),
             pltpu.VMEM((8, width), F32),
+            pltpu.VMEM((window,) + tile, BF),
+            pltpu.VMEM((window,) + tile, BF),
+            pltpu.VMEM((cells,) + tile, BF),
+            pltpu.VMEM((pairs, 8, particles), jnp.int32),
+            pltpu.SMEM((pairs, 8, particles), jnp.int32),
+            pltpu.SemaphoreType.DMA,
         ],
-        compiler_params=pltpu.CompilerParams(vmem_limit_bytes=40 << 20),
+        compiler_params=pltpu.CompilerParams(vmem_limit_bytes=56 << 20),
         name="step",
     )(*scalars, *arrays)
 

time: 140 us -> 119 us (0.85)
  blocking collectives: 56.6 us -> 40.4 us
  local copies, waits for them, and re-layouts: 7.92 us -> 3.56 us
  starting transfers between devices: 26.3 us -> 24.6 us
    all_to_all x2, blocking collectives: 56.6 us -> 40.4 us  [exchange(): lax.all_to_all(array, axis, 0, 0, axis_index_groups=groups, tiled=True)]
    unnamed x30 -> x18, local copies, waits for them, and re-layouts: 6.21 us -> 1.9 us
    ppermute x2, starting transfers between devices: 12.1 us -> 10.1 us  [swap_cores(): return lax.ppermute(array, 'wide', [(i, i ^ 1) for i in range(size)])]
where the time goes in v2:
time: 119 us; the launch traced here: 118 us
  blocking collectives  40.4 us (34%)
  Pallas kernels  40 us (34%)
  starting transfers between devices  24.6 us (21%)
  waiting for transfers between devices  6.85 us (6%)
  local copies, waits for them, and re-layouts  3.56 us (3%)
  between operations  1.5 us (1%)
  other arithmetic  1.27 us (1%)
    all_to_all x2, blocking collectives, exchange(): lax.all_to_all(array, axis, 0, 0, axis_index_groups=groups, tiled=True)  40.4 us
    pallas_call x1, Pallas kernels, run_step(): pl.pallas_call(step_kernel, grid=(1,), in_specs=[smem] * len(scalars) + [...  39.1 us
    ppermute x2, starting transfers between devices, swap_cores(): return lax.ppermute(array, 'wide', [(i, i ^ 1) for i in range(size)])  10.1 us
    ppermute x1, starting transfers between devices, on_device(): from_prev = lax.ppermute(rims[1], 'space', neighbours('space', 1))  3.99 us
    ppermute x1, starting transfers between devices, on_device(): before = lax.ppermute(last, 'space', neighbours('space', 1))  3.95 us
    all_to_all x1, starting transfers between devices, exchange(): lax.all_to_all(array, axis, 0, 0, axis_index_groups=groups, tiled=True)  3.84 us
    ppermute x1, waiting for transfers between devices, on_device(): after = lax.ppermute(initial, 'space', neighbours('space', -1))  2.73 us
  transfers between devices with their start and end apart: 7, of which 4 were waited for; matrix products, arithmetic and copies ran while one was open for 0% of the time, Pallas kernels for 0%

profile of v2, /device:TPU:1, one launch (start us, length us, event | category | flops | bytes accessed | tf_op | source)
XLA Modules:
  0.0 118.2 jit_solution(17980226591693986641)
XLA Ops:
  0.6 0.0 copy-start.8
  0.7 0.6 copy-done.8
  1.3 0.1 compare_convert_fusion
  1.4 0.0 copy-start.7
  1.4 0.1 pad.8.clone
  1.5 0.6 copy-done.7
  2.1 0.1 maximum_maximum_fusion.meta_ref
  2.1 0.0 copy-start.3
  2.1 0.8 slice_bitcast_fusion.2
  2.9 0.0 copy-done.3
  2.9 3.9 %collective-permute-start = (bf16[144,128]{1,0:T(8,128)(2,1)S(1)}, bf16[144,128]{1,0:T(8,128)(2,1)S(1)}, u32[]{:S(2)}, u32[]{:S(2)}) collective-permute-start(bf16[144,128]{1,0:T(8,128)(2,1)S(1)} %pad_maximum_fusion.1), channel_id=1, source_target_pairs={{0,32},{32,64},{64,96},{96,128},{128,160},{160,192},{192,224},{224... | collective-permute-start | bytes 110600 | tf_op jit(solution)/shard_map/ppermute | solution.py:602
  6.9 1.3 %collective-permute-start.1 = (bf16[144,128]{1,0:T(8,128)(2,1)S(1)}, bf16[144,128]{1,0:T(8,128)(2,1)S(1)}, u32[]{:S(2)}, u32[]{:S(2)}) collective-permute-start(bf16[144,128]{1,0:T(8,128)(2,1)S(1)} %pad_maximum_fusion.2), channel_id=1, source_target_pairs={{32,0},{64,32},{96,64},{128,96},{160,128},{192,160},{224,192},{256... | collective-permute-start | bytes 110600 | tf_op jit(solution)/shard_map/ppermute | solution.py:603
  8.9 0.0 collective-permute-done.before_ref
  8.9 0.0 copy-start.5
  8.9 2.7 %collective-permute-done.1.after_ref = bf16[144,128]{1,0:T(8,128)(2,1)S(1)} collective-permute-done((bf16[144,128]{1,0:T(8,128)(2,1)S(1)}, bf16[144,128]{1,0:T(8,128)(2,1)S(1)}, u32[]{:S(2)}, u32[]{:S(2)}) %collective-permute-start.1) | collective-permute-done | bytes 36896 | tf_op jit(solution)/shard_map/ppermute | solution.py:603
  11.6 0.0 copy-start.6
  11.6 0.0 copy-done.5
  11.6 0.6 copy-done.6
  12.2 39.1 %step.1 = (bf16[1,1,4,128,128]{4,3,2,1,0:T(8,128)(2,1)}, f32[1,1,4,128,128]{4,3,2,1,0:T(8,128)}, bf16[2,128,128]{2,1,0:T(8,128)(2,1)}, bf16[800,128]{1,0:T(8,128)(2,1)}) custom-call(s32[1,1,4]{2,1,0:T(1,128)} %counts_ref.1, s32[1,1,12]{2,1,0:T(1,128)} %targets_ref.1, s32[1,1,12]{2,1,0:T(1,128)} %sources_ref.1, s32[1,1]{1,0:T(1,128)S(6)} %copy.31.listed_ref, ...), custom_call_target="tpu_custom_call" | custom-call | tf_op jit(solution)/shard_map/step/pallas_call | solution.py:429
  51.3 0.0 copy-start.2
  51.3 1.0 broadcast_select_fusion
  52.3 4.0 %collective-permute-start.2 = (bf16[400,128]{1,0:T(8,128)(2,1)S(1)}, bf16[400,128]{1,0:T(8,128)(2,1)S(1)}, u32[]{:S(2)}, u32[]{:S(2)}) collective-permute-start(bf16[400,128]{1,0:T(8,128)(2,1)S(1)} %broadcast_select_fusion), channel_id=1, source_target_pairs={{0,1},{1,0},{2,3},{3,2},{4,5},{5,4},{6,7},{7,6},{8,9},{9,8},{10,11... | collective-permute-start | bytes 307208 | tf_op jit(solution)/shard_map/ppermute | solution.py:546
  56.3 0.9 collective-permute-done.2
  57.3 0.0 copy-done.2
  57.4 17.9 %all_to_all.15 = bf16[16,25,128]{2,1,0:T(8,128)(2,1)S(1)} all-to-all(bf16[16,25,128]{2,1,0:T(8,128)(2,1)S(1)} %reshape.78), channel_id=1, replica_groups=mesh['space'=16,'wide'=32] {'space'}, dimensions={0} | all-to-all | bytes 204800 | tf_op jit(solution)/shard_map/all_to_all | solution.py:550
  75.3 22.6 %all_to_all.16 = bf16[16,25,128]{2,1,0:T(8,128)(2,1)S(1)} all-to-all(bf16[16,25,128]{2,1,0:T(8,128)(2,1)S(1)} %broadcast_in_dim.38), channel_id=1, replica_groups={{0,2,4,6,8,10,12,14,16,18,20,22,24,26,28,30},{1,3,5,7,9,11,13,15,17,19,..., dimensions={0} | all-to-all | bytes 204800 | tf_op jit(solution)/shard_map/all_to_all | solution.py:550
  97.9 0.7 broadcast_in_dim.39
  98.6 0.0 copy-start.4
  98.6 3.8 %all-to-all-start.2 = ((bf16[16,25,128]{2,1,0:T(8,128)(2,1)}), bf16[16,25,128]{2,1,0:T(8,128)(2,1)S(1)}, u32[]{:S(2)}, u32[]{:S(2)}) async-start(bf16[16,25,128]{2,1,0:T(8,128)(2,1)} %broadcast_in_dim.39), calls=%async_computation.2 | async-start | bytes 262144 | tf_op jit(solution)/shard_map/all_to_all | solution.py:550
  102.4 0.0 copy-start
  102.4 0.0 copy-done.4
  102.5 1.4 %collective-permute-start.4 = (bf16[128,128]{1,0:T(8,128)(2,1)S(1)}, bf16[128,128]{1,0:T(8,128)(2,1)S(1)}, u32[]{:S(2)}, u32[]{:S(2)}) collective-permute-start(bf16[128,128]{1,0:T(8,128)(2,1)S(1)} %get-tuple-element.44), channel_id=1, source_target_pairs={{32,0},{64,32},{96,64},{128,96},{160,128},{192,160},{224,192},{256... | collective-permute-start | bytes 98312 | tf_op jit(solution)/shard_map/ppermute | solution.py:628
  103.9 4.0 %collective-permute-start.5 = (bf16[128,128]{1,0:T(8,128)(2,1)S(1)}, bf16[128,128]{1,0:T(8,128)(2,1)S(1)}, u32[]{:S(2)}, u32[]{:S(2)}) collective-permute-start(bf16[128,128]{1,0:T(8,128)(2,1)S(1)} %get-tuple-element.45), channel_id=1, source_target_pairs={{0,32},{32,64},{64,96},{96,128},{128,160},{160,192},{192,224},{224... | collective-permute-start | bytes 98312 | tf_op jit(solution)/shard_map/ppermute | solution.py:629
  107.9 2.3 %all-to-all-done.2 = bf16[16,25,128]{2,1,0:T(8,128)(2,1)S(1)} async-done(((bf16[16,25,128]{2,1,0:T(8,128)(2,1)}), bf16[16,25,128]{2,1,0:T(8,128)(2,1)S(1)}, u32[]{:S(2)}, u32[]{:S(2)}) %all-to-all-start.2) | async-done | bytes 102432 | tf_op jit(solution)/shard_map/all_to_all | solution.py:550
  110.3 6.1 %collective-permute-start.3 = (bf16[400,128]{1,0:T(8,128)(2,1)S(1)}, bf16[400,128]{1,0:T(8,128)(2,1)S(1)}, u32[]{:S(2)}, u32[]{:S(2)}) collective-permute-start(bf16[400,128]{1,0:T(8,128)(2,1)S(1)} %reshape.79.mine_ref), channel_id=1, source_target_pairs={{0,1},{1,0},{2,3},{3,2},{4,5},{5,4},{6,7},{7,6},{8,9},{9,8},{10,11... | collective-permute-start | bytes 307208 | tf_op jit(solution)/shard_map/ppermute | solution.py:546
  116.3 0.0 collective-permute-done.4
  116.3 0.0 collective-permute-done.5
  116.4 0.0 copy-start.1
  116.4 0.9 collective-permute-done.3.other_ref
  117.3 0.0 copy-done
  117.3 0.0 copy-done.1
  117.3 0.9 finish.1
  (12 shorter events, 0.3 us)
Async XLA Ops:
  0.6 0.7 copy-start.8
  1.4 0.7 copy-start.7
  2.1 0.8 copy-start.3
  2.9 5.9 %collective-permute-start = (bf16[144,128]{1,0:T(8,128)(2,1)S(1)}, bf16[144,128]{1,0:T(8,128)(2,1)S(1)}, u32[]{:S(2)}, u32[]{:S(2)}) collective-permute-start(bf16[144,128]{1,0:T(8,128)(2,1)S(1)} %pad_maximum_fusion.1), channel_id=1, source_target_pairs={{0,32},{32,64},{64,96},{96,128},{128,160},{160,192},{192,224},{224... | collective-permute-start | bytes 110600 | tf_op jit(solution)/shard_map/ppermute | solution.py:602
  6.9 4.7 %collective-permute-start.1 = (bf16[144,128]{1,0:T(8,128)(2,1)S(1)}, bf16[144,128]{1,0:T(8,128)(2,1)S(1)}, u32[]{:S(2)}, u32[]{:S(2)}) collective-permute-start(bf16[144,128]{1,0:T(8,128)(2,1)S(1)} %pad_maximum_fusion.2), channel_id=1, source_target_pairs={{32,0},{64,32},{96,64},{128,96},{160,128},{192,160},{224,192},{256... | collective-permute-start | bytes 110600 | tf_op jit(solution)/shard_map/ppermute | solution.py:603
  8.9 2.7 %copy-start.5 = (bf16[144,128]{1,0:T(8,128)(2,1)}, bf16[144,128]{1,0:T(8,128)(2,1)S(1)}, u32[]{:S(2)}) copy-start(bf16[144,128]{1,0:T(8,128)(2,1)S(1)} %collective-permute-done.before_ref) | copy-start | bytes 110596
  11.6 0.6 copy-start.6
  51.3 6.0 %copy-start.2 = (bf16[800,128]{1,0:T(8,128)(2,1)S(1)}, bf16[800,128]{1,0:T(8,128)(2,1)}, u32[]{:S(2)}) copy-start(bf16[800,128]{1,0:T(8,128)(2,1)} %get-tuple-element.28) | copy-start | bytes 614404
  52.3 5.0 %collective-permute-start.2 = (bf16[400,128]{1,0:T(8,128)(2,1)S(1)}, bf16[400,128]{1,0:T(8,128)(2,1)S(1)}, u32[]{:S(2)}, u32[]{:S(2)}) collective-permute-start(bf16[400,128]{1,0:T(8,128)(2,1)S(1)} %broadcast_select_fusion), channel_id=1, source_target_pairs={{0,1},{1,0},{2,3},{3,2},{4,5},{5,4},{6,7},{7,6},{8,9},{9,8},{10,11... | collective-permute-start | bytes 307208 | tf_op jit(solution)/shard_map/ppermute | solution.py:546
  98.6 3.9 %copy-start.4 = (bf16[2,128,128]{2,1,0:T(8,128)(2,1)S(1)}, bf16[2,128,128]{2,1,0:T(8,128)(2,1)}, u32[]{:S(2)}) copy-start(bf16[2,128,128]{2,1,0:T(8,128)(2,1)} %get-tuple-element.30) | copy-start | bytes 196612
  98.6 11.6 %all-to-all-start.2 = ((bf16[16,25,128]{2,1,0:T(8,128)(2,1)}), bf16[16,25,128]{2,1,0:T(8,128)(2,1)S(1)}, u32[]{:S(2)}, u32[]{:S(2)}) async-start(bf16[16,25,128]{2,1,0:T(8,128)(2,1)} %broadcast_in_dim.39), calls=%async_computation.2 | async-start | bytes 262144 | tf_op jit(solution)/shard_map/all_to_all | solution.py:550
  102.4 14.8 %copy-start = (f32[1,1,4,128,128]{4,3,2,1,0:T(8,128)S(1)}, f32[1,1,4,128,128]{4,3,2,1,0:T(8,128)}, u32[]{:S(2)}) copy-start(f32[1,1,4,128,128]{4,3,2,1,0:T(8,128)} %get-tuple-element.29.partial_ref) | copy-start | bytes 786436
  102.5 13.9 %collective-permute-start.4 = (bf16[128,128]{1,0:T(8,128)(2,1)S(1)}, bf16[128,128]{1,0:T(8,128)(2,1)S(1)}, u32[]{:S(2)}, u32[]{:S(2)}) collective-permute-start(bf16[128,128]{1,0:T(8,128)(2,1)S(1)} %get-tuple-element.44), channel_id=1, source_target_pairs={{32,0},{64,32},{96,64},{128,96},{160,128},{192,160},{224,192},{256... | collective-permute-start | bytes 98312 | tf_op jit(solution)/shard_map/ppermute | solution.py:628
  103.9 12.4 %collective-permute-start.5 = (bf16[128,128]{1,0:T(8,128)(2,1)S(1)}, bf16[128,128]{1,0:T(8,128)(2,1)S(1)}, u32[]{:S(2)}, u32[]{:S(2)}) collective-permute-start(bf16[128,128]{1,0:T(8,128)(2,1)S(1)} %get-tuple-element.45), channel_id=1, source_target_pairs={{0,32},{32,64},{64,96},{96,128},{128,160},{160,192},{192,224},{224... | collective-permute-start | bytes 98312 | tf_op jit(solution)/shard_map/ppermute | solution.py:629
  110.3 7.0 %collective-permute-start.3 = (bf16[400,128]{1,0:T(8,128)(2,1)S(1)}, bf16[400,128]{1,0:T(8,128)(2,1)S(1)}, u32[]{:S(2)}, u32[]{:S(2)}) collective-permute-start(bf16[400,128]{1,0:T(8,128)(2,1)S(1)} %reshape.79.mine_ref), channel_id=1, source_target_pairs={{0,1},{1,0},{2,3},{3,2},{4,5},{5,4},{6,7},{7,6},{8,9},{9,8},{10,11... | collective-permute-start | bytes 307208 | tf_op jit(solution)/shard_map/ppermute | solution.py:546
  116.4 0.9 copy-start.1

commit v3 on v2

v3 whole, which is shorter than its diff:
```python
import functools
import math
import types

import jax
import jax.numpy as jnp
from jax import lax
from jax.experimental import pallas as pl
from jax.experimental.pallas import tpu as pltpu
from jax.sharding import PartitionSpec as P

BF = jnp.bfloat16
F32 = jnp.float32
META = 16
GRAIN = 16
STEP = 16
ROWS = 64
PACK_ROWS = 800


def dot(a, b):
    return jnp.dot(a, b, preferred_element_type=F32)


def dot_t(a, b):
    return lax.dot_general(a, b, (((1,), (1,)), ((), ())), preferred_element_type=F32)


def t_dot(a, b):
    return lax.dot_general(a, b, (((0,), (0,)), ((), ())), preferred_element_type=F32)


def sigmoid(v):
    return 0.5 * (1.0 + jnp.tanh(0.5 * v))


def blocks(count, rows):
    return lax.div(count + (rows - 1), rows)


def column_sum(values):
    return jnp.sum(values, axis=0, keepdims=True)


def order_slot(s, slot, rows_in, place, target_w, bias):
    particles = place.shape[1]
    width = rows_in.shape[1]
    sub = lax.broadcasted_iota(jnp.int32, (particles, particles), 0)
    lane = lax.broadcasted_iota(jnp.int32, (particles, particles), 1)
    pick = lax.broadcasted_iota(jnp.int32, (META, width), 0)
    pick_key = jnp.where(pick == 3, 1.0, 0.0).astype(BF)
    key = jnp.where(place[2:3, :] > 0.5, place[0:1, :], 2.0)
    place = jnp.where(pick == 3, key, place).astype(BF)
    keys = t_dot(place, pick_key)
    ahead = (keys < key) | ((keys == key) & (sub < lane))
    rank = column_sum(jnp.where(ahead, 1.0, 0.0))
    order = jnp.where(sub.astype(F32) == rank, 1.0, 0.0).astype(BF)
    s.order[slot] = order
    s.place[slot] = dot_t(place, order)
    spread_place(s, slot)
    moved = s.x[slot] * s.offset[0:1, :] + (s.y[slot] - 0.5) * s.offset[1:2, :]
    rows_in = dot(order, rows_in).astype(BF)
    s.rows[slot] = rows_in
    proj_source = dot(rows_in, s.source_w[...]).astype(BF).astype(F32)
    s.b_base[slot] = 0.5 * (proj_source - moved)
    if target_w is not None:
        proj_target = (dot(rows_in, target_w[...]) + bias[...]).astype(BF)
        s.a_base[slot - 1] = 0.5 * (proj_target.astype(F32) + moved)


def spread_place(s, slot):
    pick = lax.broadcasted_iota(jnp.int32, s.place.shape[1:], 0)
    place = s.place[slot].astype(BF)
    s.x[slot] = t_dot(place, jnp.where(pick == 0, 1.0, 0.0).astype(BF))
    s.y[slot] = t_dot(place, jnp.where(pick == 1, 1.0, 0.0).astype(BF))


def pair_tools(s):
    particles, width = s.x.shape[1:]
    cells = s.a_base.shape[0]
    offset_x = s.offset[0:1, :]
    row_of = lax.broadcasted_iota(jnp.int32, (GRAIN, width), 0)
    sub = lax.broadcasted_iota(jnp.int32, (particles, particles), 0)
    listed = s.listed[0, 0]

    def pair_of(slot):
        target = s.targets[0, 0, slot]
        source = s.sources[0, 0, slot]
        off = (target - source + 1).astype(F32)
        alpha = jnp.where(off < -0.5, -1.0, jnp.where(off > 0.5, 0.0, -0.5))
        return target, source, off, alpha, off - alpha

    def bound_pair(slot, _):
        target, source, off, _, _ = pair_of(slot)
        live_target = s.live[target + 1]
        live_source = s.live[source]

        def counted(hit):
            return column_sum(jnp.where(hit, 1.0, 0.0)).astype(jnp.int32)

        x_target, row_target = s.x[target + 1], s.place[target + 1, 0:1, :]
        x_source, row_source = s.x[source], s.place[source, 0:1, :]
        zero = jnp.zeros((1, particles), jnp.int32)
        source_at_most = counted((x_source <= row_target) & (sub < live_source))
        source_below = counted((x_source < row_target) & (sub < live_source))
        target_at_most = counted((x_target <= row_source) & (sub < live_target))
        target_below = counted((x_target < row_source) & (sub < live_target))
        s.bounds[slot] = jnp.concatenate(
            [
                jnp.where(off > 0.5, source_at_most, zero),
                jnp.where(off < -0.5, source_below, zero + live_source),
                jnp.where(off < -0.5, target_at_most, zero),
                jnp.where(off > 0.5, target_below, zero + live_target),
                jnp.zeros((4, particles), jnp.int32),
            ],
            axis=0,
        )
        return 0

    def set_bounds():
        lax.fori_loop(0, listed, bound_pair, 0)
        copy = pltpu.make_async_copy(s.bounds, s.bounds_smem, s.bounds_sem)
        copy.start()
        copy.wait()

    def over_range(slot, which, first, live, visit):
        last = jnp.minimum(first + (ROWS - 1), live - 1)
        start = lax.div(s.bounds_smem[slot, which, first], STEP)
        most = particles // STEP
        size = jnp.clip(blocks(s.bounds_smem[slot, which + 1, last], STEP) - start, 0, most)
        lax.switch(
            size,
            [lambda at: None]
            + [functools.partial(visit, STEP * count) for count in range(1, most + 1)],
            jnp.clip(start, 0, most - size) * STEP,
        )

    lane_rows = lax.broadcasted_iota(jnp.int32, (GRAIN, particles), 1)

    def weights_of(x, y, there, at, first, live_here, live_there, shift):
        dx = (shift + x) - there[0:1, :]
        dy = y - there[1:2, :]
        near = jnp.maximum(1.0 - dx * dx - dy * dy, 0.0)
        keep = (row_of + first < live_here) & (lane_rows + at < live_there)
        return jnp.where(keep, near * near, 0.0).astype(BF)

    def forward_pair(slot, _):
        target, source, off, alpha, beta = pair_of(slot)
        live_target = s.live[target + 1]
        live_source = s.live[source]
        shift_a = (0.5 * alpha) * offset_x
        shift_b = (0.5 * beta) * offset_x

        def block(index, _):
            first = pl.multiple_of(index * ROWS, ROWS)

            def visit(size, at):
                at = pl.multiple_of(at, STEP)
                b = (s.b_base[source, pl.ds(at, size), :] + shift_b).astype(BF)
                there = pltpu.roll(s.place[source], particles - at, axis=1)
                for group in range(0, ROWS, GRAIN):
                    here = pl.ds(first + group, GRAIN)
                    x, y = s.x[target + 1, here, :], s.y[target + 1, here, :]
                    weights = weights_of(
                        x, y, there, at, first + group, live_target, live_source, off
                    )
                    total = jnp.zeros((GRAIN, 2 * width), F32)
                    for r in range(GRAIN):
                        a = s.a_base[target, pl.ds(first + group + r, 1), :] + shift_a
                        u = jnp.broadcast_to(a.astype(BF), (size, width)) + b
                        t = jnp.tanh(u)
                        bent = u + u * t
                        steep = 1.0 + (t + u * (1.0 - t * t))
                        one = jnp.where(row_of == r, weights, jnp.zeros_like(weights))
                        total = total + dot(
                            one[:, :size], jnp.concatenate([bent, steep], axis=1)
                        )
                    s.aggregate[target, here, :] += total[:, :width]
                    s.slope[target, here, :] += total[:, width:]
                    s.slope_shift[target, here, :] += alpha * total[:, width:]

            over_range(slot, 0, first, live_target, visit)
            return 0

        lax.fori_loop(0, blocks(live_target, ROWS), block, 0)
        return 0

    def forward(rim):
        def visit(slot, _):
            source = s.sources[0, 0, slot]
            at_rim = (source == 0) | (source == cells + 1)

            @pl.when(at_rim == rim)
            def _():
                forward_pair(slot, 0)

            return 0

        lax.fori_loop(0, listed, visit, 0)

    return pair_of, set_bounds, over_range, weights_of, forward


def own_kernel(
    counts,
    targets,
    sources,
    listed,
    latent_ref,
    meta_ref,
    target_w,
    source_w,
    offset,
    bias,
    place,
    order,
    rows,
    a_base,
    b_base,
    aggregate,
    slope,
    slope_shift,
    live,
    x,
    y,
    bounds,
    bounds_smem,
    bounds_sem,
):
    s = types.SimpleNamespace(**locals())
    cells = latent_ref.shape[2]
    live[0] = 0
    live[cells + 1] = 0
    for cell in range(cells):
        live[cell + 1] = counts[0, 0, cell]
        order_slot(
            s, cell + 1, latent_ref[0, 0, cell], meta_ref[cell].astype(F32), target_w, bias
        )
    for slot in (0, cells + 1):
        place[slot] = jnp.zeros(place.shape[1:], F32)
        order[slot] = jnp.zeros(order.shape[1:], BF)
        rows[slot] = jnp.zeros(rows.shape[1:], BF)
        b_base[slot] = jnp.zeros(b_base.shape[1:], F32)
        x[slot] = jnp.zeros(x.shape[1:], F32)
        y[slot] = jnp.zeros(y.shape[1:], F32)
    aggregate[...] = jnp.zeros_like(aggregate)
    slope[...] = jnp.zeros_like(slope)
    slope_shift[...] = jnp.zeros_like(slope_shift)
    _, set_bounds, _, _, forward = pair_tools(s)
    set_bounds()
    forward(False)


def step_kernel(
    counts,
    targets,
    sources,
    listed,
    before_ref,
    after_ref,
    cotangent_ref,
    place_in,
    order_in,
    rows_in,
    a_base,
    b_base_in,
    aggregate_in,
    slope_in,
    slope_shift_in,
    target_w,
    source_w,
    offset,
    edge_out_ref,
    node_in_ref,
    node_in_bias_ref,
    node_out_ref,
    node_out_bias_ref,
    gain_ref,
    new_latent_ref,
    latent_grad_ref,
    rim_grad_ref,
    pack_ref,
    live,
    place,
    order,
    rows,
    b_base,
    aggregate,
    slope,
    slope_shift,
    x,
    y,
    upstream_all,
    source_grad,
    shift,
    cotangent_rows,
    bounds,
    bounds_smem,
    bounds_sem,
):
    s = types.SimpleNamespace(**locals())
    s.upstream = upstream_all
    cells, particles, width = cotangent_ref.shape[2:]
    count = cells * particles
    row_of = lax.broadcasted_iota(jnp.int32, (GRAIN, width), 0)
    offset_x = offset[0:1, :]
    for cell in range(cells):
        slot = cell + 1
        live[slot] = counts[0, 0, cell]
        place[slot] = place_in[slot]
        order[slot] = order_in[slot]
        rows[slot] = rows_in[slot]
        b_base[slot] = b_base_in[slot]
        spread_place(s, slot)
        cotangent_rows[cell] = dot(order_in[slot], cotangent_ref[0, 0, cell]).astype(BF)
    for slot, rim in ((0, before_ref), (cells + 1, after_ref)):
        rim_place = rim[particles:, :].astype(F32)
        live[slot] = jnp.sum(rim_place[2:3, :]).astype(jnp.int32)
        order_slot(s, slot, rim[:particles, :], rim_place, None, None)
    aggregate[...] = aggregate_in[...]
    slope[...] = slope_in[...]
    slope_shift[...] = slope_shift_in[...]
    source_grad[...] = jnp.zeros_like(source_grad)
    shift[...] = jnp.zeros_like(shift)
    pair_of, set_bounds, over_range, weights_of, forward = pair_tools(s)
    set_bounds()
    forward(True)

    latent = s.rows[1 : cells + 1].reshape(count, width)
    agg_b = s.aggregate[...].reshape(count, width).astype(BF)
    message = dot(agg_b, edge_out_ref[...]).astype(BF)
    hidden_pre = (
        dot(latent, node_in_ref[:width, :])
        + dot(message, node_in_ref[width:, :])
        + node_in_bias_ref[...]
    )
    gate = sigmoid(hidden_pre)
    hidden_b = (hidden_pre * gate).astype(BF)
    pre_norm = dot(hidden_b, node_out_ref[...]) + node_out_bias_ref[...]
    centred = pre_norm - jnp.mean(pre_norm, axis=-1, keepdims=True)
    inverse = lax.rsqrt(jnp.mean(centred * centred, axis=-1, keepdims=True) + 1e-05)
    normed = centred * inverse
    gain = gain_ref[...]
    new_rows = (latent.astype(F32) + normed * gain).astype(BF)
    for cell in range(cells):
        there = new_rows[cell * particles : (cell + 1) * particles]
        new_latent_ref[0, 0, cell] = t_dot(s.order[cell + 1], there).astype(BF)

    cotangent = s.cotangent_rows[...].reshape(count, width).astype(F32)
    gain_sum = column_sum(cotangent * normed)
    scaled = cotangent * gain
    grad_pre = inverse * (
        scaled
        - jnp.mean(scaled, axis=-1, keepdims=True)
        - normed * jnp.mean(scaled * normed, axis=-1, keepdims=True)
    )
    grad_pre_b = grad_pre.astype(BF)
    out_bias_sum = column_sum(grad_pre)
    pack_ref[640:768, :] = t_dot(hidden_b, grad_pre_b).astype(BF)
    grad_hidden = dot_t(grad_pre_b, node_out_ref[...]) * (
        gate * (1.0 + hidden_pre * (1.0 - gate))
    )
    grad_hidden_b = grad_hidden.astype(BF)
    in_bias_sum = column_sum(grad_hidden)
    pack_ref[384:512, :] = t_dot(latent, grad_hidden_b).astype(BF)
    pack_ref[512:640, :] = t_dot(message, grad_hidden_b).astype(BF)
    grad_message = dot_t(grad_hidden_b, node_in_ref[width:, :]).astype(BF)
    pack_ref[256:384, :] = t_dot(agg_b, grad_message).astype(BF)
    upstream = dot_t(grad_message, edge_out_ref[...])
    s.upstream[...] = upstream.reshape(cells, particles, width)
    grad_rows = cotangent + dot_t(grad_hidden_b, node_in_ref[:width, :])
    s.aggregate[...] = grad_rows.reshape(cells, particles, width)

    def backward_pair(slot, _):
        target, source, off, alpha, beta = pair_of(slot)
        live_target = s.live[target + 1]
        live_source = s.live[source]
        shift_a = (0.5 * alpha) * offset_x
        shift_b = (0.5 * beta) * offset_x

        def block(index, _):
            first = pl.multiple_of(index * ROWS, ROWS)

            def visit(size, at):
                at = pl.multiple_of(at, STEP)
                a = (s.a_base[target, pl.ds(at, size), :] + shift_a).astype(BF)
                up = s.upstream[target, pl.ds(at, size), :].astype(BF)
                there = pltpu.roll(s.place[target + 1], particles - at, axis=1)

                def steep(row):
                    b = s.b_base[source, pl.ds(first + row, 1), :] + shift_b
                    u = jnp.broadcast_to(b.astype(BF), (size, width)) + a
                    t = jnp.tanh(u)
                    return up * (t + u * (1.0 - t * t))

                moved = jnp.zeros((GRAIN, width), F32)
                for group in range(0, ROWS, GRAIN):
                    here = pl.ds(first + group, GRAIN)
                    x, y = s.x[source, here, :], s.y[source, here, :]
                    weights = weights_of(
                        x, y, there, at, first + group, live_source, live_target, -off
                    )[:, :size]
                    total = jnp.zeros((GRAIN, width), F32)
                    for r in range(0, GRAIN, 2):
                        pair = jnp.concatenate([steep(group + r), steep(group + r + 1)], axis=1)
                        both = dot(weights, pair)
                        total = jnp.where(row_of == r, both[:, :width], total)
                        total = jnp.where(row_of == r + 1, both[:, width:], total)
                    total = 0.5 * (total + dot(weights, up))
                    s.source_grad[source, here, :] += total
                    moved = moved + total
                s.shift[...] += beta * (moved[:8] + moved[8:])

            over_range(slot, 2, first, live_source, visit)
            return 0

        lax.fori_loop(0, blocks(live_source, ROWS), block, 0)
        return 0

    lax.fori_loop(0, listed[0, 0], backward_pair, 0)

    upstream = s.upstream[...].reshape(count, width)
    target_grad = 0.5 * upstream * s.slope[...].reshape(count, width)
    target_b = target_grad.astype(BF)
    source_grad = s.source_grad[...].reshape(count + 2 * particles, width)
    source_b = source_grad.astype(BF)
    own_b = source_b[particles : particles + count]
    rim_grad_ref[0] = t_dot(s.order[0], source_b[:particles]).astype(BF)
    rim_grad_ref[1] = t_dot(s.order[cells + 1], source_b[particles + count :]).astype(BF)
    latent = s.rows[1 : cells + 1].reshape(count, width)
    pack_ref[0:128, :] = t_dot(latent, target_b).astype(BF)
    pack_ref[128:256, :] = (
        t_dot(latent, own_b)
        + t_dot(s.rows[0], source_b[:particles])
        + t_dot(s.rows[cells + 1], source_b[particles + count :])
    ).astype(BF)
    more = dot_t(target_b, s.target_w[...]) + dot_t(own_b, s.source_w[...])
    grad_rows = s.aggregate[...].reshape(count, width) + more
    for cell in range(cells):
        there = grad_rows[cell * particles : (cell + 1) * particles]
        coarse = there.astype(BF)
        fine = (there - coarse.astype(F32)).astype(BF)
        both = t_dot(s.order[cell + 1], jnp.concatenate([coarse, fine], axis=1))
        latent_grad_ref[0, 0, cell] = both[:, :width] + both[:, width:]
    x_target = s.x[1 : cells + 1].reshape(count, width)
    y_target = s.y[1 : cells + 1].reshape(count, width)
    x_source = s.x[...].reshape(count + 2 * particles, width)
    y_source = s.y[...].reshape(count + 2 * particles, width)
    shift = 0.5 * upstream * s.slope_shift[...].reshape(count, width)
    along = (
        column_sum(x_target * target_grad + shift)
        - column_sum(x_source * source_grad)
        + column_sum(s.shift[...])
    )
    across = column_sum((y_target - 0.5) * target_grad) - column_sum((y_source - 0.5) * source_grad)
    small = jnp.concatenate(
        [
            along,
            across,
            column_sum(target_grad),
            in_bias_sum,
            out_bias_sum,
            gain_sum,
            jnp.zeros((2, width), F32),
        ],
        axis=0,
    )
    coarse = small.astype(BF).astype(F32)
    pack_ref[768:784, :] = jnp.concatenate([coarse, small - coarse], axis=0).astype(BF)
    pack_ref[784:800, :] = jnp.zeros((16, width), BF)


def whole(array):
    return pl.BlockSpec(array.shape, lambda step: (0,) * len(array.shape))


def run_own(scalars, arrays, cells, particles, width):
    smem = pl.BlockSpec(memory_space=pltpu.SMEM)
    vmem = pl.BlockSpec(memory_space=pltpu.VMEM)
    window = cells + 2
    tile = (particles, width)
    pairs = scalars[1].shape[-1]
    outs = [
        jax.ShapeDtypeStruct((window, META, particles), F32),
        jax.ShapeDtypeStruct((window,) + tile, BF),
        jax.ShapeDtypeStruct((window,) + tile, BF),
        jax.ShapeDtypeStruct((cells,) + tile, F32),
        jax.ShapeDtypeStruct((window,) + tile, F32),
        jax.ShapeDtypeStruct((cells,) + tile, F32),
        jax.ShapeDtypeStruct((cells,) + tile, F32),
        jax.ShapeDtypeStruct((cells,) + tile, F32),
    ]
    return pl.pallas_call(
        own_kernel,
        grid=(1,),
        in_specs=[smem] * len(scalars)
        + [vmem if place == 1 else whole(array) for place, array in enumerate(arrays)],
        out_specs=[vmem] * len(outs),
        out_shape=outs,
        scratch_shapes=[
            pltpu.SMEM((window,), jnp.int32),
            pltpu.VMEM((window,) + tile, F32),
            pltpu.VMEM((window,) + tile, F32),
            pltpu.VMEM((pairs, 8, particles), jnp.int32),
            pltpu.SMEM((pairs, 8, particles), jnp.int32),
            pltpu.SemaphoreType.DMA,
        ],
        compiler_params=pltpu.CompilerParams(vmem_limit_bytes=24 << 20),
        cost_estimate=pl.CostEstimate(
            flops=1 << 31, bytes_accessed=1 << 21, transcendentals=1 << 24
        ),
        name="own",
    )(*scalars, *arrays)


def run_step(scalars, arrays, latent, cells, particles, width):
    smem = pl.BlockSpec(memory_space=pltpu.SMEM)
    vmem = pl.BlockSpec(memory_space=pltpu.VMEM)
    window = cells + 2
    tile = (particles, width)
    pairs = scalars[1].shape[-1]
    resident = (0, 1) + tuple(range(3, 11))
    outs = [
        jax.ShapeDtypeStruct(latent.shape, BF),
        jax.ShapeDtypeStruct(latent.shape, F32),
        jax.ShapeDtypeStruct((2,) + tile, BF),
        jax.ShapeDtypeStruct((PACK_ROWS, width), BF),
    ]
    return pl.pallas_call(
        step_kernel,
        grid=(1,),
        in_specs=[smem] * len(scalars)
        + [vmem if place in resident else whole(array) for place, array in enumerate(arrays)],
        out_specs=[whole(array) for array in outs[:2]] + [vmem, vmem],
        out_shape=outs,
        scratch_shapes=[
            pltpu.SMEM((window,), jnp.int32),
            pltpu.VMEM((window, META, particles), F32),
            pltpu.VMEM((window,) + tile, BF),
            pltpu.VMEM((window,) + tile, BF),
            pltpu.VMEM((window,) + tile, F32),
            pltpu.VMEM((cells,) + tile, F32),
            pltpu.VMEM((cells,) + tile, F32),
            pltpu.VMEM((cells,) + tile, F32),
            pltpu.VMEM((window,) + tile, F32),
            pltpu.VMEM((window,) + tile, F32),
            pltpu.VMEM((cells,) + tile, F32),
            pltpu.VMEM((window,) + tile, F32),
            pltpu.VMEM((8, width), F32),
            pltpu.VMEM((cells,) + tile, BF),
            pltpu.VMEM((pairs, 8, particles), jnp.int32),
            pltpu.SMEM((pairs, 8, particles), jnp.int32),
            pltpu.SemaphoreType.DMA,
        ],
        compiler_params=pltpu.CompilerParams(vmem_limit_bytes=24 << 20),
        name="step",
    )(*scalars, *arrays)


def finish_kernel(
    core_ref,
    mine_ref,
    other_ref,
    partial_ref,
    rims_ref,
    source_w_ref,
    latent_grad_ref,
    target_w_out,
    source_w_out,
    offset_out,
    bias_out,
    edge_out_out,
    node_in_out,
    in_bias_out,
    node_out_out,
    out_bias_out,
    gain_out,
    *,
    scale,
):
    cells = partial_ref.shape[2]
    mine = mine_ref[...].astype(F32)
    other = other_ref[...].astype(F32)
    first = core_ref[0] == 0
    low = jnp.where(first, mine, other) * scale
    high = jnp.where(first, other, mine) * scale
    whole = jnp.concatenate([low, high], axis=0)
    target_w_out[...] = whole[0:128]
    source_w_out[...] = whole[128:256]
    edge_out_out[...] = whole[256:384]
    node_in_out[...] = whole[384:640]
    node_out_out[...] = whole[640:768]
    small = whole[768:776] + whole[776:784]
    offset_out[...] = small[0:2]
    bias_out[...] = small[2:3]
    in_bias_out[...] = small[3:4]
    out_bias_out[...] = small[4:5]
    gain_out[...] = small[5:6]
    latent_grad_ref[...] = partial_ref[...]
    latent_grad_ref[0, 0, cells - 1] += dot_t(rims_ref[0], source_w_ref[...])
    latent_grad_ref[0, 0, 0] += dot_t(rims_ref[1], source_w_ref[...])


def run_finish(core, mine, other, partial, rims, source_w, scale):
    width = mine.shape[-1]
    vmem = pl.BlockSpec(memory_space=pltpu.VMEM)
    smem = pl.BlockSpec(memory_space=pltpu.SMEM)
    square = jax.ShapeDtypeStruct((width, width), F32)
    row = jax.ShapeDtypeStruct((1, width), F32)
    return pl.pallas_call(
        functools.partial(finish_kernel, scale=scale),
        in_specs=[smem] + [vmem] * 5,
        out_specs=[vmem] * 11,
        out_shape=[
            jax.ShapeDtypeStruct(partial.shape, F32),
            square,
            square,
            jax.ShapeDtypeStruct((2, width), F32),
            row,
            square,
            jax.ShapeDtypeStruct((2 * width, width), F32),
            row,
            square,
            row,
            row,
        ],
        compiler_params=pltpu.CompilerParams(vmem_limit_bytes=32 << 20),
        name="finish",
    )(core, mine, other, partial, rims, source_w)


def neighbours(axis, by):
    length = lax.axis_size(axis)
    return [(i, i + by) for i in range(length) if 0 <= i + by < length]


def swap_cores(array):
    size = lax.axis_size("wide")
    return lax.ppermute(array, "wide", [(i, i ^ 1) for i in range(size)])


def exchange(array, axis, groups=None):
    return lax.all_to_all(array, axis, 0, 0, axis_index_groups=groups, tiled=True)


def spread(array, count):
    return jnp.broadcast_to(array[None], (count,) + array.shape)


def sum_everywhere(pack, core, first):
    width = pack.shape[-1]
    space = lax.axis_size("space")
    wide = lax.axis_size("wide")
    fellows = [list(range(start, wide, 2)) for start in range(2)]
    halves = pack.reshape(2, -1, width)
    mine = jnp.where(core == 0, halves[0], halves[1])
    sent = jnp.where(core == 0, halves[1], halves[0])
    half = mine.astype(F32) + swap_cores(sent).astype(F32)
    parts = half.astype(BF).reshape(space, -1, width)
    parts, *first = lax.optimization_barrier((parts,) + first)
    part = jnp.sum(exchange(parts, "space").astype(F32), axis=0).astype(BF)
    others = exchange(spread(part, wide // 2), "wide", fellows)
    part = jnp.sum(others.astype(F32), axis=0).astype(BF)
    return exchange(spread(part, space), "space").reshape(-1, width), *first


def on_device(
    latent,
    coords,
    cell_counts,
    pair_target,
    pair_source,
    pair_count,
    edge_target_w,
    edge_source_w,
    edge_offset,
    edge_bias,
    edge_out,
    node_in,
    node_in_bias,
    node_out,
    node_out_bias,
    norm_gain,
    cotangent,
):
    cells, particles, width = latent.shape[2:]
    core = lax.rem(lax.axis_index("wide"), 2)
    live = (
        jnp.arange(particles, dtype=jnp.int32)[None, :] < cell_counts[0, 0][:, None]
    ).astype(BF)
    meta = jnp.concatenate(
        [coords[0, 0], live[:, None, :], jnp.zeros((cells, META - 3, particles), BF)], axis=1
    )
    last = jnp.concatenate([latent[0, 0, cells - 1], meta[cells - 1]], axis=0)
    initial = jnp.concatenate([latent[0, 0, 0], meta[0]], axis=0)
    before = lax.ppermute(last, "space", neighbours("space", 1))
    after = lax.ppermute(initial, "space", neighbours("space", -1))
    scalars = (cell_counts, pair_target, pair_source, pair_count)
    state = run_own(
        scalars,
        (latent, meta, edge_target_w, edge_source_w, edge_offset, edge_bias[None, :]),
        cells,
        particles,
        width,
    )
    new_rows, partial, rims, pack = run_step(
        scalars,
        (before, after, cotangent)
        + tuple(state)
        + (
            edge_target_w,
            edge_source_w,
            edge_offset,
            edge_out,
            node_in,
            node_in_bias[None, :],
            node_out,
            node_out_bias[None, :],
            norm_gain[None, :],
        ),
        latent,
        cells,
        particles,
        width,
    )
    from_next = lax.ppermute(rims[0], "space", neighbours("space", -1))
    from_prev = lax.ppermute(rims[1], "space", neighbours("space", 1))
    mine, from_next, from_prev = sum_everywhere(pack, core, (from_next, from_prev))
    other = swap_cores(mine)
    scale = 1.0 / math.sqrt(lax.axis_size("space") * lax.axis_size("wide") * cells * particles)
    rims_in = jnp.stack([from_next, from_prev])
    outs = run_finish(
        core.astype(jnp.int32)[None], mine, other, partial, rims_in, edge_source_w, scale
    )
    (latent_grad, target_w, source_w, offset, bias, out_w, in_w, in_bias, node_w, out_bias, gain) = outs
    return (
        new_rows,
        latent_grad,
        target_w,
        source_w,
        offset,
        bias[0],
        out_w,
        in_w,
        in_bias[0],
        node_w,
        out_bias[0],
        gain[0],
    )


def solution(mesh):
    cell = P("wide", "space", None, None, None)
    table = P("wide", "space", None)
    return jax.shard_map(
        on_device,
        mesh=mesh,
        in_specs=(cell, cell, table, table, table, P("wide", "space")) + (P(),) * 10 + (cell,),
        out_specs=(cell, cell) + (P(),) * 10,
        check_vma=False,
    )
```

time: 119 us -> 125 us (1.050)
  blocking collectives: 40.4 us -> 63.1 us
  Pallas kernels: 40 us -> 18.9 us
  starting transfers between devices: 24.6 us -> 35.5 us
  waiting for transfers between devices: 6.85 us -> 1.8 us
    pallas_call x1, Pallas kernels: 39.1 us -> 10 us  [run_step(): pl.pallas_call(step_kernel, grid=(1,), in_specs=[smem] * len(scalars) + [...]
    all_to_all x2 -> x3, blocking collectives: 40.4 us -> 63.1 us  [exchange(): lax.all_to_all(array, axis, 0, 0, axis_index_groups=groups, tiled=True)]
    ppermute x1, starting transfers between devices: 3.99 us -> 15.2 us  [on_device(): from_prev = lax.ppermute(rims[1], 'space', neighbours('space', 1))]
    pallas_call x0 -> x1, Pallas kernels: none -> 7.94 us  [run_own(): pl.pallas_call(own_kernel, grid=(1,), in_specs=[smem] * len(scalars) + [v...]
    all_to_all x1 -> x0, starting transfers between devices: 3.84 us -> none  [exchange(): lax.all_to_all(array, axis, 0, 0, axis_index_groups=groups, tiled=True)]
    ppermute x2, starting transfers between devices: 10.1 us -> 13.7 us  [swap_cores(): return lax.ppermute(array, 'wide', [(i, i ^ 1) for i in range(size)])]
    ppermute x1, waiting for transfers between devices: 2.73 us -> 0.01 us  [on_device(): after = lax.ppermute(initial, 'space', neighbours('space', -1))]
    all_to_all x1 -> x0, waiting for transfers between devices: 2.31 us -> none  [exchange(): lax.all_to_all(array, axis, 0, 0, axis_index_groups=groups, tiled=True)]
  transfers between devices with their start and end apart: 7 -> 6, of which waited for: 4 -> 2; matrix products, arithmetic and copies ran while one was open for 0% -> 0% of each run, Pallas kernels for 0% -> 6%
where the time goes in v3:
time: 125 us
  blocking collectives  63.1 us (50%)
  starting transfers between devices  35.5 us (28%)
  Pallas kernels  18.9 us (15%)
  local copies, waits for them, and re-layouts  3.65 us (3%)
  waiting for transfers between devices  1.8 us (1%)
  between operations  1.62 us (1%)
    all_to_all x3, blocking collectives, exchange(): lax.all_to_all(array, axis, 0, 0, axis_index_groups=groups, tiled=True)  63.1 us
    ppermute x1, starting transfers between devices, on_device(): from_prev = lax.ppermute(rims[1], 'space', neighbours('space', 1))  15.2 us
    ppermute x2, starting transfers between devices, swap_cores(): return lax.ppermute(array, 'wide', [(i, i ^ 1) for i in range(size)])  13.7 us
    pallas_call x1, Pallas kernels, run_step(): pl.pallas_call(step_kernel, grid=(1,), in_specs=[smem] * len(scalars) + [...  10 us
    pallas_call x1, Pallas kernels, run_own(): pl.pallas_call(own_kernel, grid=(1,), in_specs=[smem] * len(scalars) + [v...  7.94 us
    ppermute x1, starting transfers between devices, on_device(): before = lax.ppermute(last, 'space', neighbours('space', 1))  3.95 us
    unnamed x32, local copies, waits for them, and re-layouts  2.59 us
  transfers between devices with their start and end apart: 6, of which 2 were waited for; matrix products, arithmetic and copies ran while one was open for 0% of the time, Pallas kernels for 6%

profile of v3, /device:TPU:1, one launch (start us, length us, event | category | flops | bytes accessed | tf_op | source)
XLA Modules:
  0.0 124.9 jit_solution(10505088997359539321)
XLA Ops:
  0.6 0.0 copy-start.7
  0.7 0.6 copy-done.7
  1.3 0.1 compare_convert_fusion
  1.4 0.1 pad.8.clone
  1.5 0.6 copy-done.15
  2.1 0.1 maximum_maximum_fusion.meta_ref
  2.1 0.8 slice_bitcast_fusion.2
  3.0 3.9 %collective-permute-start = (bf16[144,128]{1,0:T(8,128)(2,1)S(1)}, bf16[144,128]{1,0:T(8,128)(2,1)S(1)}, u32[]{:S(2)}, u32[]{:S(2)}) collective-permute-start(bf16[144,128]{1,0:T(8,128)(2,1)S(1)} %pad_maximum_fusion.1), channel_id=1, source_target_pairs={{0,32},{32,64},{64,96},{96,128},{128,160},{160,192},{192,224},{224... | collective-permute-start | bytes 110600 | tf_op jit(solution)/shard_map/ppermute | solution.py:696
  6.9 0.0 copy-start
  7.0 0.0 copy-start.3
  7.0 0.0 copy-start.10
  7.0 0.0 copy-start.14
  7.0 1.3 %collective-permute-start.1 = (bf16[144,128]{1,0:T(8,128)(2,1)S(1)}, bf16[144,128]{1,0:T(8,128)(2,1)S(1)}, u32[]{:S(2)}, u32[]{:S(2)}) collective-permute-start(bf16[144,128]{1,0:T(8,128)(2,1)S(1)} %pad_maximum_fusion.2), channel_id=1, source_target_pairs={{32,0},{64,32},{96,64},{128,96},{160,128},{192,160},{224,192},{256... | collective-permute-start | bytes 110600 | tf_op jit(solution)/shard_map/ppermute | solution.py:697
  9.0 0.0 copy-start.8
  9.0 0.0 copy-start.9
  9.0 0.0 copy-done.6
  9.0 0.0 copy-done
  9.0 0.0 copy-done.3
  9.0 0.0 copy-done.10
  9.0 0.0 copy-done.14
  9.0 0.6 copy-done.8
  9.6 0.0 copy-done.9
  9.6 7.9 %own.1 = (f32[6,16,128]{2,1,0:T(8,128)S(1)}, bf16[6,128,128]{2,1,0:T(8,128)(2,1)S(1)}, bf16[6,128,128]{2,1,0:T(8,128)(2,1)S(1)}, f32[4,128,128]{2,1,0:T(8,128)S(...) custom-call(s32[1,1,4]{2,1,0:T(1,128)S(1)} %copy-done.7, ...), custom_call_target="tpu_custom_call" | custom-call | flops 2147483648 | bytes 2097152 | tf_op jit(solution)/shard_map/own/pallas_call | solution.py:493
  17.6 0.0 copy-start.4
  17.6 0.0 collective-permute-done.before_ref
  17.6 0.0 collective-permute-done.1.after_ref
  17.6 0.0 copy-start.11
  17.6 0.0 copy-start.12
  17.7 0.0 copy-start.13
  17.7 0.0 copy-done.1
  17.7 0.0 copy-done.2
  17.7 0.0 copy-done.5
  17.7 0.7 copy-done.4
  18.4 0.0 copy-done.11
  18.4 0.0 copy-done.12
  18.4 10.0 %step.1 = (bf16[1,1,4,128,128]{4,3,2,1,0:T(8,128)(2,1)}, f32[1,1,4,128,128]{4,3,2,1,0:T(8,128)S(1)}, bf16[2,128,128]{2,1,0:T(8,128)(2,1)S(1)}, bf16[800,128]{1,0:T(8,128)(2,1)S(1)}) custom-call(s32[1,1,4]{2,1,0:T(1,128)S(1)} %copy-done.7, s32[1,1,12]{2,1,0:T(1,128)S(1)} %copy-done.9, s32[1,1,12]{2,1,0:T(1,128)S(1)} %copy-done.10, s32[1,1]{1,0:T(1,128)S(6)} %copy.31.listed, ...), custom_call_target="tpu_custom_call" | custom-call | tf_op jit(solution)/shard_map/step/pallas_call | solution.py:529
  28.4 6.8 %collective-permute-start.2 = (bf16[400,128]{1,0:T(8,128)(2,1)S(1)}, bf16[400,128]{1,0:T(8,128)(2,1)S(1)}, u32[]{:S(2)}, u32[]{:S(2)}) collective-permute-start(bf16[400,128]{1,0:T(8,128)(2,1)S(1)} %broadcast_select_fusion), channel_id=1, source_target_pairs={{0,1},{1,0},{2,3},{3,2},{4,5},{5,4},{6,7},{7,6},{8,9},{9,8},{10,11... | collective-permute-start | bytes 307208 | tf_op jit(solution)/shard_map/ppermute | solution.py:639
  35.2 1.3 %collective-permute-start.3 = (bf16[128,128]{1,0:T(8,128)(2,1)S(1)}, bf16[128,128]{1,0:T(8,128)(2,1)S(1)}, u32[]{:S(2)}, u32[]{:S(2)}) collective-permute-start(bf16[128,128]{1,0:T(8,128)(2,1)S(1)} %get-tuple-element.67), channel_id=1, source_target_pairs={{32,0},{64,32},{96,64},{128,96},{160,128},{192,160},{224,192},{256... | collective-permute-start | bytes 98312 | tf_op jit(solution)/shard_map/ppermute | solution.py:726
  36.5 15.2 %collective-permute-start.4 = (bf16[128,128]{1,0:T(8,128)(2,1)S(1)}, bf16[128,128]{1,0:T(8,128)(2,1)S(1)}, u32[]{:S(2)}, u32[]{:S(2)}) collective-permute-start(bf16[128,128]{1,0:T(8,128)(2,1)S(1)} %get-tuple-element.66), channel_id=1, source_target_pairs={{0,32},{32,64},{64,96},{96,128},{128,160},{160,192},{192,224},{224... | collective-permute-start | bytes 98312 | tf_op jit(solution)/shard_map/ppermute | solution.py:727
  51.8 0.0 collective-permute-done.2
  51.9 0.0 collective-permute-done.3
  51.9 0.9 collective-permute-done.4
  52.8 22.9 %all_to_all.15 = bf16[16,25,128]{2,1,0:T(8,128)(2,1)S(1)} all-to-all(bf16[16,25,128]{2,1,0:T(8,128)(2,1)S(1)} %reshape.78), channel_id=1, replica_groups=mesh['space'=16,'wide'=32] {'space'}, dimensions={0} | all-to-all | bytes 204800 | tf_op jit(solution)/shard_map/all_to_all | solution.py:643
  75.7 29.9 %all_to_all.16 = bf16[16,25,128]{2,1,0:T(8,128)(2,1)S(1)} all-to-all(bf16[16,25,128]{2,1,0:T(8,128)(2,1)S(1)} %broadcast_in_dim.38), channel_id=1, replica_groups={{0,2,4,6,8,10,12,14,16,18,20,22,24,26,28,30},{1,3,5,7,9,11,13,15,17,19,..., dimensions={0} | all-to-all | bytes 204800 | tf_op jit(solution)/shard_map/all_to_all | solution.py:643
  105.6 10.4 %all_to_all.17 = bf16[16,25,128]{2,1,0:T(8,128)(2,1)S(1)} all-to-all(bf16[16,25,128]{2,1,0:T(8,128)(2,1)S(1)} %broadcast_in_dim.39), channel_id=1, replica_groups=mesh['space'=16,'wide'=32] {'space'}, dimensions={0} | all-to-all | bytes 204800 | tf_op jit(solution)/shard_map/all_to_all | solution.py:643
  116.0 7.0 %collective-permute-start.5 = (bf16[400,128]{1,0:T(8,128)(2,1)S(1)}, bf16[400,128]{1,0:T(8,128)(2,1)S(1)}, u32[]{:S(2)}, u32[]{:S(2)}) collective-permute-start(bf16[400,128]{1,0:T(8,128)(2,1)S(1)} %reshape.79.mine_ref), channel_id=1, source_target_pairs={{0,1},{1,0},{2,3},{3,2},{4,5},{5,4},{6,7},{7,6},{8,9},{9,8},{10,11... | collective-permute-start | bytes 307208 | tf_op jit(solution)/shard_map/ppermute | solution.py:639
  123.1 0.9 collective-permute-done.5.other_ref
  124.0 0.9 finish.1
  (20 shorter events, 0.3 us)
Async XLA Ops:
  0.6 0.7 copy-start.7
  1.4 0.7 copy-start.15
  2.1 6.8 %copy-start.6 = (bf16[1,1,4,128,128]{4,3,2,1,0:T(8,128)(2,1)S(1)}, bf16[1,1,4,128,128]{4,3,2,1,0:T(8,128)(2,1)}, u32[]{:S(2)}) copy-start(bf16[1,1,4,128,128]{4,3,2,1,0:T(8,128)(2,1)} %latent_ref.1) | copy-start | bytes 393220
  3.0 14.6 %collective-permute-start = (bf16[144,128]{1,0:T(8,128)(2,1)S(1)}, bf16[144,128]{1,0:T(8,128)(2,1)S(1)}, u32[]{:S(2)}, u32[]{:S(2)}) collective-permute-start(bf16[144,128]{1,0:T(8,128)(2,1)S(1)} %pad_maximum_fusion.1), channel_id=1, source_target_pairs={{0,32},{32,64},{64,96},{96,128},{128,160},{160,192},{192,224},{224... | collective-permute-start | bytes 110600 | tf_op jit(solution)/shard_map/ppermute | solution.py:696
  6.9 2.0 %copy-start = (bf16[128,128]{1,0:T(8,128)(2,1)S(1)}, bf16[128,128]{1,0:T(8,128)(2,1)}, u32[]{:S(2)}) copy-start(bf16[128,128]{1,0:T(8,128)(2,1)} %source_w_ref.1) | copy-start | bytes 98308
  7.0 2.0 %copy-start.3 = (bf16[128,128]{1,0:T(8,128)(2,1)S(1)}, bf16[128,128]{1,0:T(8,128)(2,1)}, u32[]{:S(2)}) copy-start(bf16[128,128]{1,0:T(8,128)(2,1)} %target_w.3) | copy-start | bytes 98308
  7.0 2.0 %copy-start.10 = (s32[1,1,12]{2,1,0:T(1,128)S(1)}, s32[1,1,12]{2,1,0:T(1,128)}, u32[]{:S(2)}) copy-start(s32[1,1,12]{2,1,0:T(1,128)} %sources.3) | copy-start | bytes 148
  7.0 2.0 %copy-start.14 = (f32[128]{0:T(128)S(1)}, f32[128]{0:T(128)}, u32[]{:S(2)}) copy-start(f32[128]{0:T(128)} %param.26) | copy-start | bytes 1540
  7.0 10.6 %collective-permute-start.1 = (bf16[144,128]{1,0:T(8,128)(2,1)S(1)}, bf16[144,128]{1,0:T(8,128)(2,1)S(1)}, u32[]{:S(2)}, u32[]{:S(2)}) collective-permute-start(bf16[144,128]{1,0:T(8,128)(2,1)S(1)} %pad_maximum_fusion.2), channel_id=1, source_target_pairs={{32,0},{64,32},{96,64},{128,96},{160,128},{192,160},{224,192},{256... | collective-permute-start | bytes 110600 | tf_op jit(solution)/shard_map/ppermute | solution.py:697
  9.0 0.7 copy-start.8
  9.0 0.7 copy-start.9
  9.6 8.0 %copy-start.1 = (bf16[1,1,4,128,128]{4,3,2,1,0:T(8,128)(2,1)S(1)}, bf16[1,1,4,128,128]{4,3,2,1,0:T(8,128)(2,1)}, u32[]{:S(2)}) copy-start(bf16[1,1,4,128,128]{4,3,2,1,0:T(8,128)(2,1)} %cotangent_ref.1) | copy-start | bytes 393220
  9.6 8.0 %copy-start.2 = (bf16[256,128]{1,0:T(8,128)(2,1)S(1)}, bf16[256,128]{1,0:T(8,128)(2,1)}, u32[]{:S(2)}) copy-start(bf16[256,128]{1,0:T(8,128)(2,1)} %node_in_ref.1) | copy-start | bytes 196612
  9.6 8.1 %copy-start.5 = (bf16[128,128]{1,0:T(8,128)(2,1)S(1)}, bf16[128,128]{1,0:T(8,128)(2,1)}, u32[]{:S(2)}) copy-start(bf16[128,128]{1,0:T(8,128)(2,1)} %node_out_ref.1) | copy-start | bytes 98308
  17.6 0.8 copy-start.4
  17.6 0.7 copy-start.11
  17.6 0.7 copy-start.12
  17.7 0.7 copy-start.13
  28.4 23.3 %collective-permute-start.2 = (bf16[400,128]{1,0:T(8,128)(2,1)S(1)}, bf16[400,128]{1,0:T(8,128)(2,1)S(1)}, u32[]{:S(2)}, u32[]{:S(2)}) collective-permute-start(bf16[400,128]{1,0:T(8,128)(2,1)S(1)} %broadcast_select_fusion), channel_id=1, source_target_pairs={{0,1},{1,0},{2,3},{3,2},{4,5},{5,4},{6,7},{7,6},{8,9},{9,8},{10,11... | collective-permute-start | bytes 307208 | tf_op jit(solution)/shard_map/ppermute | solution.py:639
  35.2 16.7 %collective-permute-start.3 = (bf16[128,128]{1,0:T(8,128)(2,1)S(1)}, bf16[128,128]{1,0:T(8,128)(2,1)S(1)}, u32[]{:S(2)}, u32[]{:S(2)}) collective-permute-start(bf16[128,128]{1,0:T(8,128)(2,1)S(1)} %get-tuple-element.67), channel_id=1, source_target_pairs={{32,0},{64,32},{96,64},{128,96},{160,128},{192,160},{224,192},{256... | collective-permute-start | bytes 98312 | tf_op jit(solution)/shard_map/ppermute | solution.py:726
  36.5 16.3 %collective-permute-start.4 = (bf16[128,128]{1,0:T(8,128)(2,1)S(1)}, bf16[128,128]{1,0:T(8,128)(2,1)S(1)}, u32[]{:S(2)}, u32[]{:S(2)}) collective-permute-start(bf16[128,128]{1,0:T(8,128)(2,1)S(1)} %get-tuple-element.66), channel_id=1, source_target_pairs={{0,32},{32,64},{64,96},{96,128},{128,160},{160,192},{192,224},{224... | collective-permute-start | bytes 98312 | tf_op jit(solution)/shard_map/ppermute | solution.py:727
  116.0 7.9 %collective-permute-start.5 = (bf16[400,128]{1,0:T(8,128)(2,1)S(1)}, bf16[400,128]{1,0:T(8,128)(2,1)S(1)}, u32[]{:S(2)}, u32[]{:S(2)}) collective-permute-start(bf16[400,128]{1,0:T(8,128)(2,1)S(1)} %reshape.79.mine_ref), channel_id=1, source_target_pairs={{0,1},{1,0},{2,3},{3,2},{4,5},{5,4},{6,7},{7,6},{8,9},{9,8},{10,11... | collective-permute-start | bytes 307208 | tf_op jit(solution)/shard_map/ppermute | solution.py:639

commit v4 on v3

--- a/solution.py
+++ b/solution.py
@@ -117,8 +117,21 @@
         )
         return 0
 
-    def set_bounds():
-        lax.fori_loop(0, listed, bound_pair, 0)
+    def over_pairs(rim, pair):
+        def visit(slot, _):
+            source = s.sources[0, 0, slot]
+            at_rim = (source == 0) | (source == cells + 1)
+
+            @pl.when(at_rim == rim)
+            def _():
+                pair(slot, 0)
+
+            return 0
+
+        lax.fori_loop(0, listed, visit, 0)
+
+    def set_bounds(rim):
+        over_pairs(rim, bound_pair)
         copy = pltpu.make_async_copy(s.bounds, s.bounds_smem, s.bounds_sem)
         copy.start()
         copy.wait()
@@ -186,17 +199,7 @@
         return 0
 
     def forward(rim):
-        def visit(slot, _):
-            source = s.sources[0, 0, slot]
-            at_rim = (source == 0) | (source == cells + 1)
-
-            @pl.when(at_rim == rim)
-            def _():
-                forward_pair(slot, 0)
-
-            return 0
-
-        lax.fori_loop(0, listed, visit, 0)
+        over_pairs(rim, forward_pair)
 
     return pair_of, set_bounds, over_range, weights_of, forward
 
@@ -220,10 +223,10 @@
     aggregate,
     slope,
     slope_shift,
+    bounds,
     live,
     x,
     y,
-    bounds,
     bounds_smem,
     bounds_sem,
 ):
@@ -247,7 +250,8 @@
     slope[...] = jnp.zeros_like(slope)
     slope_shift[...] = jnp.zeros_like(slope_shift)
     _, set_bounds, _, _, forward = pair_tools(s)
-    set_bounds()
+    bounds[...] = jnp.zeros_like(bounds)
+    set_bounds(False)
     forward(False)
 
 
@@ -267,6 +271,7 @@
     aggregate_in,
     slope_in,
     slope_shift_in,
+    bounds_in,
     target_w,
     source_w,
     offset,
@@ -323,7 +328,8 @@
     source_grad[...] = jnp.zeros_like(source_grad)
     shift[...] = jnp.zeros_like(shift)
     pair_of, set_bounds, over_range, weights_of, forward = pair_tools(s)
-    set_bounds()
+    bounds[...] = bounds_in[...]
+    set_bounds(True)
     forward(True)
 
     latent = s.rows[1 : cells + 1].reshape(count, width)
@@ -489,6 +495,7 @@
         jax.ShapeDtypeStruct((cells,) + tile, F32),
         jax.ShapeDtypeStruct((cells,) + tile, F32),
         jax.ShapeDtypeStruct((cells,) + tile, F32),
+        jax.ShapeDtypeStruct((pairs, 8, particles), jnp.int32),
     ]
     return pl.pallas_call(
         own_kernel,
@@ -501,7 +508,6 @@
             pltpu.SMEM((window,), jnp.int32),
             pltpu.VMEM((window,) + tile, F32),
             pltpu.VMEM((window,) + tile, F32),
-            pltpu.VMEM((pairs, 8, particles), jnp.int32),
             pltpu.SMEM((pairs, 8, particles), jnp.int32),
             pltpu.SemaphoreType.DMA,
         ],
@@ -519,7 +525,7 @@
     window = cells + 2
     tile = (particles, width)
     pairs = scalars[1].shape[-1]
-    resident = (0, 1) + tuple(range(3, 11))
+    resident = (0, 1) + tuple(range(3, 12))
     outs = [
         jax.ShapeDtypeStruct(latent.shape, BF),
         jax.ShapeDtypeStruct(latent.shape, F32),
@@ -651,7 +657,8 @@
     width = pack.shape[-1]
     space = lax.axis_size("space")
     wide = lax.axis_size("wide")
-    fellows = [list(range(start, wide, 2)) for start in range(2)]
+    columns = [list(range(start, wide, 4)) for start in range(4)]
+    across = [(i, i ^ 2) for i in range(wide)]
     halves = pack.reshape(2, -1, width)
     mine = jnp.where(core == 0, halves[0], halves[1])
     sent = jnp.where(core == 0, halves[1], halves[0])
@@ -659,7 +666,8 @@
     parts = half.astype(BF).reshape(space, -1, width)
     parts, *first = lax.optimization_barrier((parts,) + first)
     part = jnp.sum(exchange(parts, "space").astype(F32), axis=0).astype(BF)
-    others = exchange(spread(part, wide // 2), "wide", fellows)
+    part = (part.astype(F32) + lax.ppermute(part, "wide", across).astype(F32)).astype(BF)
+    others = exchange(spread(part, wide // 4), "wide", columns)
     part = jnp.sum(others.astype(F32), axis=0).astype(BF)
     return exchange(spread(part, space), "space").reshape(-1, width), *first
 

time: 125 us -> 126 us (level); the launches traced: 125 us -> 127 us
  blocking collectives: 63.1 us -> 50.2 us
  starting transfers between devices: 35.5 us -> 47.8 us
  Pallas kernels: 18.9 us -> 21 us
    ppermute x2, starting transfers between devices: 13.7 us -> 27.9 us  [swap_cores(): return lax.ppermute(array, 'wide', [(i, i ^ 1) for i in range(size)])]
    all_to_all x3, blocking collectives: 63.1 us -> 50.2 us  [exchange(): lax.all_to_all(array, axis, 0, 0, axis_index_groups=groups, tiled=True)]
    ppermute x1, starting transfers between devices: 15.2 us -> 3.99 us  [on_device(): from_prev = lax.ppermute(rims[1], 'space', neighbours('space', 1))]
    ppermute x0 -> x1, starting transfers between devices: none -> 9.33 us  [sum_everywhere(): lax.ppermute(part, 'wide', across).astype(F32)]
    pallas_call x1, Pallas kernels: 7.94 us -> 9.22 us  [run_own(): pl.pallas_call(own_kernel, grid=(1,), in_specs=[smem] * len(scalars) + [v...]
  transfers between devices with their start and end apart: 6 -> 7, of which waited for: 2 -> 3; matrix products, arithmetic and copies ran while one was open for 0% -> 0% of each run, Pallas kernels for 6% -> 7%
where the time goes in v4:
time: 126 us; the launch traced here: 127 us
  blocking collectives  50.2 us (40%)
  starting transfers between devices  47.8 us (38%)
  Pallas kernels  21 us (17%)
  local copies, waits for them, and re-layouts  3.64 us (3%)
  waiting for transfers between devices  2.82 us (2%)
  between operations  1.63 us (1%)
    all_to_all x3, blocking collectives, exchange(): lax.all_to_all(array, axis, 0, 0, axis_index_groups=groups, tiled=True)  50.2 us
    ppermute x2, starting transfers between devices, swap_cores(): return lax.ppermute(array, 'wide', [(i, i ^ 1) for i in range(size)])  27.9 us
    pallas_call x1, Pallas kernels, run_step(): pl.pallas_call(step_kernel, grid=(1,), in_specs=[smem] * len(scalars) + [...  10.8 us
    ppermute x1, starting transfers between devices, sum_everywhere(): lax.ppermute(part, 'wide', across).astype(F32)  9.33 us
    pallas_call x1, Pallas kernels, run_own(): pl.pallas_call(own_kernel, grid=(1,), in_specs=[smem] * len(scalars) + [v...  9.22 us
    ppermute x1, starting transfers between devices, on_device(): from_prev = lax.ppermute(rims[1], 'space', neighbours('space', 1))  3.99 us
    ppermute x1, starting transfers between devices, on_device(): before = lax.ppermute(last, 'space', neighbours('space', 1))  3.95 us
    unnamed x32, local copies, waits for them, and re-layouts  2.59 us
  transfers between devices with their start and end apart: 7, of which 3 were waited for; matrix products, arithmetic and copies ran while one was open for 0% of the time, Pallas kernels for 7%

profile of v4, /device:TPU:1, one launch (start us, length us, event | category | flops | bytes accessed | tf_op | source)
XLA Modules:
  0.0 127.3 jit_solution(10824687418654183354)
XLA Ops:
  0.6 0.0 copy-start.7
  0.7 0.6 copy-done.7
  1.3 0.1 compare_convert_fusion
  1.4 0.1 pad.8.clone
  1.5 0.6 copy-done.15
  2.1 0.1 maximum_maximum_fusion.meta_ref
  2.1 0.8 slice_bitcast_fusion.2
  3.0 3.9 %collective-permute-start = (bf16[144,128]{1,0:T(8,128)(2,1)S(1)}, bf16[144,128]{1,0:T(8,128)(2,1)S(1)}, u32[]{:S(2)}, u32[]{:S(2)}) collective-permute-start(bf16[144,128]{1,0:T(8,128)(2,1)S(1)} %pad_maximum_fusion.1), channel_id=1, source_target_pairs={{0,32},{32,64},{64,96},{96,128},{128,160},{160,192},{192,224},{224... | collective-permute-start | bytes 110600 | tf_op jit(solution)/shard_map/ppermute | solution.py:704
  6.9 0.0 copy-start
  7.0 0.0 copy-start.3
  7.0 0.0 copy-start.10
  7.0 0.0 copy-start.14
  7.0 1.3 %collective-permute-start.1 = (bf16[144,128]{1,0:T(8,128)(2,1)S(1)}, bf16[144,128]{1,0:T(8,128)(2,1)S(1)}, u32[]{:S(2)}, u32[]{:S(2)}) collective-permute-start(bf16[144,128]{1,0:T(8,128)(2,1)S(1)} %pad_maximum_fusion.2), channel_id=1, source_target_pairs={{32,0},{64,32},{96,64},{128,96},{160,128},{192,160},{224,192},{256... | collective-permute-start | bytes 110600 | tf_op jit(solution)/shard_map/ppermute | solution.py:705
  9.0 0.0 copy-start.8
  9.0 0.0 copy-start.9
  9.0 0.0 copy-done.6
  9.0 0.0 copy-done
  9.0 0.0 copy-done.3
  9.0 0.0 copy-done.10
  9.0 0.0 copy-done.14
  9.0 0.6 copy-done.8
  9.6 0.0 copy-done.9
  9.6 9.2 %own.1 = (f32[6,16,128]{2,1,0:T(8,128)S(1)}, bf16[6,128,128]{2,1,0:T(8,128)(2,1)S(1)}, bf16[6,128,128]{2,1,0:T(8,128)(2,1)S(1)}, f32[4,128,128]{2,1,0:T(8,128)S(...) custom-call(s32[1,1,4]{2,1,0:T(1,128)S(1)} %copy-done.7, ...), custom_call_target="tpu_custom_call" | custom-call | flops 2147483648 | bytes 2097152 | tf_op jit(solution)/shard_map/own/pallas_call | solution.py:500
  18.9 0.0 copy-start.4
  18.9 0.0 collective-permute-done.before_ref
  18.9 0.0 collective-permute-done.1.after_ref
  18.9 0.0 copy-start.11
  18.9 0.0 copy-start.12
  18.9 0.0 copy-start.13
  18.9 0.0 copy-done.1
  19.0 0.0 copy-done.2
  19.0 0.7 copy-done.4
  19.6 0.0 copy-done.12
  19.6 10.8 %step.1 = (bf16[1,1,4,128,128]{4,3,2,1,0:T(8,128)(2,1)}, f32[1,1,4,128,128]{4,3,2,1,0:T(8,128)S(1)}, bf16[2,128,128]{2,1,0:T(8,128)(2,1)S(1)}, bf16[800,128]{1,0:T(8,128)(2,1)S(1)}) custom-call(s32[1,1,4]{2,1,0:T(1,128)S(1)} %copy-done.7, s32[1,1,12]{2,1,0:T(1,128)S(1)} %copy-done.9, s32[1,1,12]{2,1,0:T(1,128)S(1)} %copy-done.10, s32[1,1]{1,0:T(1,128)S(6)} %copy.31.listed, ...), custom_call_target="tpu_custom_call" | custom-call | tf_op jit(solution)/shard_map/step/pallas_call | solution.py:535
  30.5 19.7 %collective-permute-start.2 = (bf16[400,128]{1,0:T(8,128)(2,1)S(1)}, bf16[400,128]{1,0:T(8,128)(2,1)S(1)}, u32[]{:S(2)}, u32[]{:S(2)}) collective-permute-start(bf16[400,128]{1,0:T(8,128)(2,1)S(1)} %broadcast_select_fusion), channel_id=1, source_target_pairs={{0,1},{1,0},{2,3},{3,2},{4,5},{5,4},{6,7},{7,6},{8,9},{9,8},{10,11... | collective-permute-start | bytes 307208 | tf_op jit(solution)/shard_map/ppermute | solution.py:645
  50.2 1.3 %collective-permute-start.3 = (bf16[128,128]{1,0:T(8,128)(2,1)S(1)}, bf16[128,128]{1,0:T(8,128)(2,1)S(1)}, u32[]{:S(2)}, u32[]{:S(2)}) collective-permute-start(bf16[128,128]{1,0:T(8,128)(2,1)S(1)} %get-tuple-element.69), channel_id=1, source_target_pairs={{32,0},{64,32},{96,64},{128,96},{160,128},{192,160},{224,192},{256... | collective-permute-start | bytes 98312 | tf_op jit(solution)/shard_map/ppermute | solution.py:734
  51.5 4.0 %collective-permute-start.4 = (bf16[128,128]{1,0:T(8,128)(2,1)S(1)}, bf16[128,128]{1,0:T(8,128)(2,1)S(1)}, u32[]{:S(2)}, u32[]{:S(2)}) collective-permute-start(bf16[128,128]{1,0:T(8,128)(2,1)S(1)} %get-tuple-element.68), channel_id=1, source_target_pairs={{0,32},{32,64},{64,96},{96,128},{128,160},{160,192},{192,224},{224... | collective-permute-start | bytes 98312 | tf_op jit(solution)/shard_map/ppermute | solution.py:735
  55.5 0.0 collective-permute-done.2
  55.6 0.0 collective-permute-done.3
  55.6 0.9 collective-permute-done.4
  56.5 21.8 %all_to_all.15 = bf16[16,25,128]{2,1,0:T(8,128)(2,1)S(1)} all-to-all(bf16[16,25,128]{2,1,0:T(8,128)(2,1)S(1)} %reshape.78), channel_id=1, replica_groups=mesh['space'=16,'wide'=32] {'space'}, dimensions={0} | all-to-all | bytes 204800 | tf_op jit(solution)/shard_map/all_to_all | solution.py:649
  78.4 9.3 %collective-permute-start.5 = (bf16[25,128]{1,0:T(8,128)(2,1)S(1)}, bf16[25,128]{1,0:T(8,128)(2,1)S(1)}, u32[]{:S(2)}, u32[]{:S(2)}) collective-permute-start(bf16[25,128]{1,0:T(8,128)(2,1)S(1)} %reduce_sum.24), channel_id=1, source_target_pairs={{0,2},{1,3},{2,0},{3,1},{4,6},{5,7},{6,4},{7,5},{8,10},{9,11},{10,... | collective-permute-start | bytes 19208 | tf_op jit(solution)/shard_map/ppermute | solution.py:669
  87.7 1.0 collective-permute-done.5
  88.8 18.0 %all_to_all.16 = bf16[8,25,128]{2,1,0:T(8,128)(2,1)S(1)} all-to-all(bf16[8,25,128]{2,1,0:T(8,128)(2,1)S(1)} %broadcast_in_dim.38), channel_id=1, replica_groups={{0,4,8,12,16,20,24,28},{1,5,9,13,17,21,25,29},{2,6,10,14,18,22,26,30},{..., dimensions={0} | all-to-all | bytes 102400 | tf_op jit(solution)/shard_map/all_to_all | solution.py:649
  106.8 10.4 %all_to_all.17 = bf16[16,25,128]{2,1,0:T(8,128)(2,1)S(1)} all-to-all(bf16[16,25,128]{2,1,0:T(8,128)(2,1)S(1)} %broadcast_in_dim.39), channel_id=1, replica_groups=mesh['space'=16,'wide'=32] {'space'}, dimensions={0} | all-to-all | bytes 204800 | tf_op jit(solution)/shard_map/all_to_all | solution.py:649
  117.3 8.2 %collective-permute-start.6 = (bf16[400,128]{1,0:T(8,128)(2,1)S(1)}, bf16[400,128]{1,0:T(8,128)(2,1)S(1)}, u32[]{:S(2)}, u32[]{:S(2)}) collective-permute-start(bf16[400,128]{1,0:T(8,128)(2,1)S(1)} %reshape.79.mine_ref), channel_id=1, source_target_pairs={{0,1},{1,0},{2,3},{3,2},{4,5},{5,4},{6,7},{7,6},{8,9},{9,8},{10,11... | collective-permute-start | bytes 307208 | tf_op jit(solution)/shard_map/ppermute | solution.py:645
  125.5 0.9 collective-permute-done.6.other_ref
  126.4 0.9 finish.1
  (23 shorter events, 0.3 us)
Async XLA Ops:
  0.6 0.7 copy-start.7
  1.4 0.7 copy-start.15
  2.1 6.8 %copy-start.6 = (bf16[1,1,4,128,128]{4,3,2,1,0:T(8,128)(2,1)S(1)}, bf16[1,1,4,128,128]{4,3,2,1,0:T(8,128)(2,1)}, u32[]{:S(2)}) copy-start(bf16[1,1,4,128,128]{4,3,2,1,0:T(8,128)(2,1)} %latent_ref.1) | copy-start | bytes 393220
  3.0 15.9 %collective-permute-start = (bf16[144,128]{1,0:T(8,128)(2,1)S(1)}, bf16[144,128]{1,0:T(8,128)(2,1)S(1)}, u32[]{:S(2)}, u32[]{:S(2)}) collective-permute-start(bf16[144,128]{1,0:T(8,128)(2,1)S(1)} %pad_maximum_fusion.1), channel_id=1, source_target_pairs={{0,32},{32,64},{64,96},{96,128},{128,160},{160,192},{192,224},{224... | collective-permute-start | bytes 110600 | tf_op jit(solution)/shard_map/ppermute | solution.py:704
  6.9 2.0 %copy-start = (bf16[128,128]{1,0:T(8,128)(2,1)S(1)}, bf16[128,128]{1,0:T(8,128)(2,1)}, u32[]{:S(2)}) copy-start(bf16[128,128]{1,0:T(8,128)(2,1)} %source_w_ref.1) | copy-start | bytes 98308
  7.0 2.0 %copy-start.3 = (bf16[128,128]{1,0:T(8,128)(2,1)S(1)}, bf16[128,128]{1,0:T(8,128)(2,1)}, u32[]{:S(2)}) copy-start(bf16[128,128]{1,0:T(8,128)(2,1)} %target_w.3) | copy-start | bytes 98308
  7.0 2.0 %copy-start.10 = (s32[1,1,12]{2,1,0:T(1,128)S(1)}, s32[1,1,12]{2,1,0:T(1,128)}, u32[]{:S(2)}) copy-start(s32[1,1,12]{2,1,0:T(1,128)} %sources.3) | copy-start | bytes 148
  7.0 2.0 %copy-start.14 = (f32[128]{0:T(128)S(1)}, f32[128]{0:T(128)}, u32[]{:S(2)}) copy-start(f32[128]{0:T(128)} %param.26) | copy-start | bytes 1540
  7.0 11.9 %collective-permute-start.1 = (bf16[144,128]{1,0:T(8,128)(2,1)S(1)}, bf16[144,128]{1,0:T(8,128)(2,1)S(1)}, u32[]{:S(2)}, u32[]{:S(2)}) collective-permute-start(bf16[144,128]{1,0:T(8,128)(2,1)S(1)} %pad_maximum_fusion.2), channel_id=1, source_target_pairs={{32,0},{64,32},{96,64},{128,96},{160,128},{192,160},{224,192},{256... | collective-permute-start | bytes 110600 | tf_op jit(solution)/shard_map/ppermute | solution.py:705
  9.0 0.7 copy-start.8
  9.0 0.7 copy-start.9
  9.6 9.3 %copy-start.1 = (bf16[1,1,4,128,128]{4,3,2,1,0:T(8,128)(2,1)S(1)}, bf16[1,1,4,128,128]{4,3,2,1,0:T(8,128)(2,1)}, u32[]{:S(2)}) copy-start(bf16[1,1,4,128,128]{4,3,2,1,0:T(8,128)(2,1)} %cotangent_ref.1) | copy-start | bytes 393220
  9.6 9.3 %copy-start.2 = (bf16[256,128]{1,0:T(8,128)(2,1)S(1)}, bf16[256,128]{1,0:T(8,128)(2,1)}, u32[]{:S(2)}) copy-start(bf16[256,128]{1,0:T(8,128)(2,1)} %node_in_ref.1) | copy-start | bytes 196612
  9.6 9.3 %copy-start.5 = (bf16[128,128]{1,0:T(8,128)(2,1)S(1)}, bf16[128,128]{1,0:T(8,128)(2,1)}, u32[]{:S(2)}) copy-start(bf16[128,128]{1,0:T(8,128)(2,1)} %node_out_ref.1) | copy-start | bytes 98308
  18.9 0.8 copy-start.4
  18.9 0.7 copy-start.11
  18.9 0.7 copy-start.12
  18.9 0.7 copy-start.13
  30.5 25.0 %collective-permute-start.2 = (bf16[400,128]{1,0:T(8,128)(2,1)S(1)}, bf16[400,128]{1,0:T(8,128)(2,1)S(1)}, u32[]{:S(2)}, u32[]{:S(2)}) collective-permute-start(bf16[400,128]{1,0:T(8,128)(2,1)S(1)} %broadcast_select_fusion), channel_id=1, source_target_pairs={{0,1},{1,0},{2,3},{3,2},{4,5},{5,4},{6,7},{7,6},{8,9},{9,8},{10,11... | collective-permute-start | bytes 307208 | tf_op jit(solution)/shard_map/ppermute | solution.py:645
  50.2 5.4 %collective-permute-start.3 = (bf16[128,128]{1,0:T(8,128)(2,1)S(1)}, bf16[128,128]{1,0:T(8,128)(2,1)S(1)}, u32[]{:S(2)}, u32[]{:S(2)}) collective-permute-start(bf16[128,128]{1,0:T(8,128)(2,1)S(1)} %get-tuple-element.69), channel_id=1, source_target_pairs={{32,0},{64,32},{96,64},{128,96},{160,128},{192,160},{224,192},{256... | collective-permute-start | bytes 98312 | tf_op jit(solution)/shard_map/ppermute | solution.py:734
  51.5 5.0 %collective-permute-start.4 = (bf16[128,128]{1,0:T(8,128)(2,1)S(1)}, bf16[128,128]{1,0:T(8,128)(2,1)S(1)}, u32[]{:S(2)}, u32[]{:S(2)}) collective-permute-start(bf16[128,128]{1,0:T(8,128)(2,1)S(1)} %get-tuple-element.68), channel_id=1, source_target_pairs={{0,32},{32,64},{64,96},{96,128},{128,160},{160,192},{192,224},{224... | collective-permute-start | bytes 98312 | tf_op jit(solution)/shard_map/ppermute | solution.py:735
  78.4 10.4 %collective-permute-start.5 = (bf16[25,128]{1,0:T(8,128)(2,1)S(1)}, bf16[25,128]{1,0:T(8,128)(2,1)S(1)}, u32[]{:S(2)}, u32[]{:S(2)}) collective-permute-start(bf16[25,128]{1,0:T(8,128)(2,1)S(1)} %reduce_sum.24), channel_id=1, source_target_pairs={{0,2},{1,3},{2,0},{3,1},{4,6},{5,7},{6,4},{7,5},{8,10},{9,11},{10,... | collective-permute-start | bytes 19208 | tf_op jit(solution)/shard_map/ppermute | solution.py:669
  117.3 9.1 %collective-permute-start.6 = (bf16[400,128]{1,0:T(8,128)(2,1)S(1)}, bf16[400,128]{1,0:T(8,128)(2,1)S(1)}, u32[]{:S(2)}, u32[]{:S(2)}) collective-permute-start(bf16[400,128]{1,0:T(8,128)(2,1)S(1)} %reshape.79.mine_ref), channel_id=1, source_target_pairs={{0,1},{1,0},{2,3},{3,2},{4,5},{5,4},{6,7},{7,6},{8,9},{9,8},{10,11... | collective-permute-start | bytes 307208 | tf_op jit(solution)/shard_map/ppermute | solution.py:645
